TPU v7x, 32 devices: a whole 2x2x4 slice. The times are simulated.
32 devices in a mesh: parts: 2 (over y), tile: 4 (over z), shot: 4 (over x, core).
Axes of the slice: x: 2, y: 2, z: 4, core: 2. Of those that a mesh axis runs over, the one named last changes fastest.
Arguments:
- velocity: bfloat16 [128, 32, 128], P(('parts', 'tile'), 'shot'), parts along dimension 0, may hold values from 0.14941406 to 0.44921875
- density: bfloat16 [128, 32, 128], P(('parts', 'tile'), 'shot'), parts along dimension 0, may hold values from 1.796875 to 2.59375
- wave_now: bfloat16 [8, 64, 32, 128], P(('parts', 'shot'), 'tile'), parts along dimension 0, may hold values from -6 to 6
- wave_before: bfloat16 [8, 64, 32, 128], P(('parts', 'shot'), 'tile'), parts along dimension 0, may hold values from -6 to 6
- adjoint_end: bfloat16 [8, 64, 32, 128], P(('parts', 'shot'), 'tile'), parts along dimension 0, may hold values from -6 to 6
- adjoint_after: bfloat16 [8, 64, 32, 128], P(('parts', 'shot'), 'tile'), parts along dimension 0, may hold values from -6 to 6
- source_cell: int32 [8], P(('parts', 'shot')), parts along dimension 0, may hold values from 0 to 262143, as said below
- source_wave: float32 [8, 4], P(('parts', 'shot')), parts along dimension 0, may hold values from -8 to 8
- receiver_cell: int32 [8, 256], P(('parts', 'shot')), parts along dimension 0, may hold values from 0 to 262143, as said below
- residual_traces: float32 [8, 4, 256], P(('parts', 'shot')), parts along dimension 0, may hold values from -6 to 6
- aperture: int32 [8, 2], P(('parts', 'shot')), parts along dimension 0, may hold values from -1 to 3, as said below
Outputs:
- gradient: float32 [128, 32, 128], P(('parts', 'tile'), 'shot'), parts along dimension 0
- wave_end: bfloat16 [8, 64, 32, 128], P(('parts', 'shot'), 'tile'), parts along dimension 0
- adjoint_start: bfloat16 [8, 64, 32, 128], P(('parts', 'shot'), 'tile'), parts along dimension 0
There are 2 independent parts, one for each index of `parts`. A program takes and returns all parts, laid end to end along the dimension named above; each array names one. Nothing has to cross between parts.
Inputs may be any that keep to these rules, and one draw needn't show every extreme that they name: `aperture`: row s lists a run of consecutive tile numbers, 1 to 2 of them, followed by -1 entries. `source_cell`: the flat index x * 32 * 128 + y * 128 + z of the shot's source cell, whose x lies in a tile of the shot's aperture. `receiver_cell`: flat indices as for source_cell, each in a tile of the shot's aperture; a cell may repeat.
All inputs are finite; a program needn't handle non-finite values.
Results may differ from a plain program's by a relative error of at most 0.001.
Values may be sent and summed in bfloat16 or wider, within the bound.
No kernel may reach another device: no remote copies, remote signals or barrier semaphores. Data moves between devices by JAX's collectives and lax.ppermute only.
A program may use at most 64 MiB of HBM per device.

v0:
```python
import jax
import jax.numpy as jnp
from jax import lax
from jax.sharding import PartitionSpec as P

SECOND_COEFFS = (-205.0 / 72.0, 8.0 / 5.0, -1.0 / 5.0, 8.0 / 315.0, -1.0 / 560.0)
FIRST_COEFFS = (4.0 / 5.0, -1.0 / 5.0, 4.0 / 105.0, -1.0 / 280.0)


def extended_2(shard, sides, width):
    for axis, dim in sides:
        size, length = (lax.axis_size(axis), shard.shape[dim])
        up = [(i, (i + 1) % size) for i in range(size - 1)]
        down = [(j, i) for i, j in up]
        last = lax.slice_in_dim(shard, length - width, length, axis=dim)
        initial = lax.slice_in_dim(shard, 0, width, axis=dim)
        before = lax.ppermute(last, axis, up)
        after = lax.ppermute(initial, axis, down)
        shard = jnp.concatenate([before, shard, after], axis=dim)
    return shard


def shifted(padded, which_axis, offset_cells):
    leading = padded.ndim - 3
    starts = [0] * padded.ndim
    limits = list(padded.shape)
    for position in range(3):
        starts[leading + position] = 4
        limits[leading + position] = padded.shape[leading + position] - 4
    starts[leading + which_axis] += offset_cells
    limits[leading + which_axis] += offset_cells
    return lax.slice(padded, starts, limits)


def first_diff(padded, which_axis):
    result = 0.0
    for offset_cells in range(1, 5):
        result = result + FIRST_COEFFS[offset_cells - 1] * (
            shifted(padded, which_axis, offset_cells) - shifted(padded, which_axis, -offset_cells)
        )
    return result


def operate(padded, slopes):
    summed = 3.0 * SECOND_COEFFS[0] * shifted(padded, 0, 0)
    for which_axis in range(3):
        second_term = 0.0
        first_term = 0.0
        for offset_cells in range(1, 5):
            plus_side = shifted(padded, which_axis, offset_cells)
            minus_side = shifted(padded, which_axis, -offset_cells)
            second_term = second_term + SECOND_COEFFS[offset_cells] * (plus_side + minus_side)
            first_term = first_term + FIRST_COEFFS[offset_cells - 1] * (plus_side - minus_side)
        summed = summed + second_term - slopes[which_axis] * first_term
    return summed


def pad_sides(field):
    widths = [(0, 0)] * (field.ndim - 2) + [(4, 4), (4, 4)]
    return jnp.pad(field, widths)


def inject(field, cells, values, offset, count_cells):
    local_cell = cells - offset
    inside = (local_cell >= 0) & (local_cell < count_cells)
    local_cell = jnp.where(inside, local_cell, count_cells)
    flat_field = field.reshape(field.shape[0], count_cells)
    slot_rows = jnp.broadcast_to(
        jnp.arange(field.shape[0], dtype=jnp.int32)[:, None], local_cell.shape
    )
    flat_field = flat_field.at[slot_rows, local_cell].add(values, mode="drop")
    return flat_field.reshape(field.shape)


def local(
    velocity,
    density,
    wave_now,
    wave_before,
    adjoint_end,
    adjoint_after,
    source_cell,
    source_wave,
    receiver_cell,
    residual_traces,
    aperture,
):
    speed_tile, density_tile = (
        lax.all_gather(velocity, "shot", axis=1, tiled=True),
        lax.all_gather(density, "shot", axis=1, tiled=True),
    )
    speed_cells = speed_tile.astype(jnp.float32)
    courant_sq = speed_cells * speed_cells
    density_ext = extended_2(density_tile, (("tile", 0),), 4).astype(jnp.float32)
    log_density = jnp.log(jnp.where(density_ext > 0.0, density_ext, 1.0))
    padded_log = pad_sides(log_density)
    slopes = tuple((first_diff(padded_log, which_axis) for which_axis in range(3)))
    tile_here = lax.axis_index("tile")
    count_cells = speed_cells.size
    offset = tile_here * count_cells
    active = jnp.any(aperture == tile_here, axis=1).astype(jnp.float32)[:, None, None, None]
    num_steps = source_wave.shape[1]
    previous = wave_before.astype(jnp.float32)
    current = wave_now.astype(jnp.float32)
    adjoint_later = adjoint_after.astype(jnp.float32)
    adjoint = adjoint_end.astype(jnp.float32)
    stored = []
    for step_index in range(num_steps):
        extended = extended_2(current, (("tile", 1),), 4)
        applied = operate(pad_sides(extended), slopes)
        forward_next = 2.0 * current - previous + courant_sq * applied
        forward_next = (
            inject(
                forward_next,
                source_cell[:, None],
                source_wave[:, step_index][:, None],
                offset,
                count_cells,
            )
            * active
        )
        stored.append(applied)
        previous, current = (current, forward_next)
    imaging = jnp.zeros_like(current)
    for step_index in range(num_steps, 0, -1):
        extended = extended_2(adjoint, (("tile", 1),), 4)
        applied = operate(pad_sides(extended), slopes)
        adjoint_next = 2.0 * adjoint - adjoint_later + courant_sq * applied
        adjoint_next = (
            inject(
                adjoint_next,
                receiver_cell,
                residual_traces[:, step_index - 1, :],
                offset,
                count_cells,
            )
            * active
        )
        imaging = imaging + adjoint_next * stored[step_index - 1]
        adjoint_later, adjoint = (adjoint, adjoint_next)
    local_term = 2.0 * speed_cells * jnp.sum(imaging, axis=0)
    gradient = lax.psum_scatter(local_term, "shot", scatter_dimension=1, tiled=True)
    return (gradient, current.astype(jnp.bfloat16), adjoint.astype(jnp.bfloat16))


def solution(mesh):
    placed = (
        P(("parts", "tile"), "shot", None),
        P(("parts", "tile"), "shot", None),
        P(("parts", "shot"), "tile", None, None),
        P(("parts", "shot"), "tile", None, None),
        P(("parts", "shot"), "tile", None, None),
        P(("parts", "shot"), "tile", None, None),
        P(("parts", "shot")),
        P(("parts", "shot"), None),
        P(("parts", "shot"), None),
        P(("parts", "shot"), None, None),
        P(("parts", "shot"), None),
    )
    return jax.shard_map(
        local,
        mesh=mesh,
        in_specs=placed,
        out_specs=(
            P(("parts", "tile"), "shot", None),
            P(("parts", "shot"), "tile", None, None),
            P(("parts", "shot"), "tile", None, None),
        ),
        check_vma=False,
    )
```

profile of v0, /device:TPU:16, one launch (start us, length us, event | category | flops | bytes accessed | tf_op | source)
XLA Modules:
  0.0 141.9 jit_solution(3275329687525224547)
XLA Ops:
  8.0 2.4 %collective-permute-start.4 = (f32[1,4,32,128]{3,2,1,0:T(8,128)S(1)}, f32[1,4,32,128]{3,2,1,0:T(8,128)S(1)}, u32[]{:S(2)}, u32[]{:S(2)}) collective-permute-start(f32[1,4,32,128]{3,2,1,0:T(8,128)S(1)} %get-tuple-element.79), channel_id=1, source_target_pairs={{4,0},{8,4},{12,8},{5,1},{9,5},{13,9},{6,2},{10,6},{14,10},{7,3},{... | collective-permute-start | bytes 196616 | tf_op jit(solution)/shard_map/ppermute | solution.py:18
  10.4 3.6 %collective-permute-start.5 = (f32[1,4,32,128]{3,2,1,0:T(8,128)S(1)}, f32[1,4,32,128]{3,2,1,0:T(8,128)S(1)}, u32[]{:S(2)}, u32[]{:S(2)}) collective-permute-start(f32[1,4,32,128]{3,2,1,0:T(8,128)S(1)} %get-tuple-element.78), channel_id=1, source_target_pairs={{0,4},{4,8},{8,12},{1,5},{5,9},{9,13},{2,6},{6,10},{10,14},{3,7},{... | collective-permute-start | bytes 196616 | tf_op jit(solution)/shard_map/ppermute | solution.py:17
  14.0 5.4 %all_gather.7 = bf16[16,32,128]{2,1,0:T(8,128)(2,1)S(1)} all-gather(bf16[16,8,128]{2,1,0:T(8,128)(2,1)S(1)} %copy-done.4), channel_id=1, replica_groups=mesh['parts'=2,'tile'=4,'shot'=4] {'shot'}, dimensions={1}, use_global_device_ids=true | all-gather | bytes 163840 | tf_op jit(solution)/shard_map/all_gather | solution.py:90
  21.4 4.1 %collective-permute-start.3 = (bf16[4,32,128]{2,1,0:T(8,128)(2,1)S(1)}, bf16[4,32,128]{2,1,0:T(8,128)(2,1)S(1)}, u32[]{:S(2)}, u32[]{:S(2)}) collective-permute-start(bf16[4,32,128]{2,1,0:T(8,128)(2,1)S(1)} %get-tuple-element.77), channel_id=1, source_target_pairs={{4,0},{8,4},{12,8},{5,1},{9,5},{13,9},{6,2},{10,6},{14,10},{7,3},{... | collective-permute-start | bytes 98312 | tf_op jit(solution)/shard_map/ppermute | solution.py:18
  25.5 2.4 %collective-permute-start = (f32[1,4,32,128]{3,2,1,0:T(8,128)S(1)}, f32[1,4,32,128]{3,2,1,0:T(8,128)S(1)}, u32[]{:S(2)}, u32[]{:S(2)}) collective-permute-start(f32[1,4,32,128]{3,2,1,0:T(8,128)S(1)} %get-tuple-element.75), channel_id=1, source_target_pairs={{4,0},{8,4},{12,8},{5,1},{9,5},{13,9},{6,2},{10,6},{14,10},{7,3},{... | collective-permute-start | bytes 196616 | tf_op jit(solution)/shard_map/ppermute | solution.py:18
  32.6 5.4 %all_gather.6 = bf16[16,32,128]{2,1,0:T(8,128)(2,1)S(1)} all-gather(bf16[16,8,128]{2,1,0:T(8,128)(2,1)S(1)} %copy-done.5), channel_id=1, replica_groups=mesh['parts'=2,'tile'=4,'shot'=4] {'shot'}, dimensions={1}, use_global_device_ids=true | all-gather | bytes 163840 | tf_op jit(solution)/shard_map/all_gather | solution.py:89
  38.1 3.5 %collective-permute-start.1 = (f32[1,4,32,128]{3,2,1,0:T(8,128)S(1)}, f32[1,4,32,128]{3,2,1,0:T(8,128)S(1)}, u32[]{:S(2)}, u32[]{:S(2)}) collective-permute-start(f32[1,4,32,128]{3,2,1,0:T(8,128)S(1)} %get-tuple-element.74), channel_id=1, source_target_pairs={{0,4},{4,8},{8,12},{1,5},{5,9},{9,13},{2,6},{6,10},{10,14},{3,7},{... | collective-permute-start | bytes 196616 | tf_op jit(solution)/shard_map/ppermute | solution.py:17
  42.5 2.3 %fusion.15 = (f32[1,16,32,128]{3,2,1,0:T(8,128)S(1)}, f32[1,16,32,128]{3,2,1,0:T(8,128)S(1)}, f32[1,16,32,128]{3,2,1,0:T(8,128)S(1)}, f32[1,16,32,128]{3,2,1,0:T(8,128)S(1)}, f32[1,16,32,128]{3,2,1,0:T(8,128)S(1)}) fusion(bf16[16,32,128]{2,1,0:T(8,128)(2,1)S(1)} %all_gather.6, bf16[1,16,32,128]{3,2,1,0:T(8,128)(2,1)S(1)} %copy-done.2, ...), kind=kLoop, calls=%fused_computation.154 | loop fusion | flops 8192000 | bytes 8781824 | tf_op jit(solution)/shard_map/add | solution.py:111
  48.3 2.4 %collective-permute-start.6 = (f32[1,4,32,128]{3,2,1,0:T(8,128)S(1)}, f32[1,4,32,128]{3,2,1,0:T(8,128)S(1)}, u32[]{:S(2)}, u32[]{:S(2)}) collective-permute-start(f32[1,4,32,128]{3,2,1,0:T(8,128)S(1)} %get-tuple-element.67), channel_id=1, source_target_pairs={{4,0},{8,4},{12,8},{5,1},{9,5},{13,9},{6,2},{10,6},{14,10},{7,3},{... | collective-permute-start | bytes 196616 | tf_op jit(solution)/shard_map/ppermute | solution.py:18
  50.7 3.6 %collective-permute-start.7 = (f32[1,4,32,128]{3,2,1,0:T(8,128)S(1)}, f32[1,4,32,128]{3,2,1,0:T(8,128)S(1)}, u32[]{:S(2)}, u32[]{:S(2)}) collective-permute-start(f32[1,4,32,128]{3,2,1,0:T(8,128)S(1)} %get-tuple-element.66), channel_id=1, source_target_pairs={{0,4},{4,8},{8,12},{1,5},{5,9},{9,13},{2,6},{6,10},{10,14},{3,7},{... | collective-permute-start | bytes 196616 | tf_op jit(solution)/shard_map/ppermute | solution.py:17
  55.8 2.1 %scatter_fusion = f32[65536]{0:T(1024)S(1)} fusion(f32[65536]{0:T(1024)S(1)} %bitcast.77, s32[256]{0:T(256)S(1)} %bitcast.116, f32[256]{0:T(256)S(1)} %bitcast.123), kind=kCustom, calls=%fused_computation | custom fusion | flops 256 | bytes 4096 | tf_op jit(solution)/shard_map/scatter-add | solution.py:71
  57.9 2.4 %collective-permute-start.12 = (f32[1,4,32,128]{3,2,1,0:T(8,128)S(1)}, f32[1,4,32,128]{3,2,1,0:T(8,128)S(1)}, u32[]{:S(2)}, u32[]{:S(2)}) collective-permute-start(f32[1,4,32,128]{3,2,1,0:T(8,128)S(1)} %get-tuple-element.73), channel_id=1, source_target_pairs={{4,0},{8,4},{12,8},{5,1},{9,5},{13,9},{6,2},{10,6},{14,10},{7,3},{... | collective-permute-start | bytes 196616 | tf_op jit(solution)/shard_map/ppermute | solution.py:18
  60.3 3.5 %collective-permute-start.13 = (f32[1,4,32,128]{3,2,1,0:T(8,128)S(1)}, f32[1,4,32,128]{3,2,1,0:T(8,128)S(1)}, u32[]{:S(2)}, u32[]{:S(2)}) collective-permute-start(f32[1,4,32,128]{3,2,1,0:T(8,128)S(1)} %get-tuple-element.72), channel_id=1, source_target_pairs={{0,4},{4,8},{8,12},{1,5},{5,9},{9,13},{2,6},{6,10},{10,14},{3,7},{... | collective-permute-start | bytes 196616 | tf_op jit(solution)/shard_map/ppermute | solution.py:17
  68.8 2.4 %collective-permute-start.8 = (f32[1,4,32,128]{3,2,1,0:T(8,128)S(1)}, f32[1,4,32,128]{3,2,1,0:T(8,128)S(1)}, u32[]{:S(2)}, u32[]{:S(2)}) collective-permute-start(f32[1,4,32,128]{3,2,1,0:T(8,128)S(1)} %get-tuple-element.65), channel_id=1, source_target_pairs={{4,0},{8,4},{12,8},{5,1},{9,5},{13,9},{6,2},{10,6},{14,10},{7,3},{... | collective-permute-start | bytes 196616 | tf_op jit(solution)/shard_map/ppermute | solution.py:18
  71.1 3.5 %collective-permute-start.9 = (f32[1,4,32,128]{3,2,1,0:T(8,128)S(1)}, f32[1,4,32,128]{3,2,1,0:T(8,128)S(1)}, u32[]{:S(2)}, u32[]{:S(2)}) collective-permute-start(f32[1,4,32,128]{3,2,1,0:T(8,128)S(1)} %get-tuple-element.64), channel_id=1, source_target_pairs={{0,4},{4,8},{8,12},{1,5},{5,9},{9,13},{2,6},{6,10},{10,14},{3,7},{... | collective-permute-start | bytes 196616 | tf_op jit(solution)/shard_map/ppermute | solution.py:17
  76.1 2.1 %scatter_fusion.1 = f32[65536]{0:T(1024)S(1)} fusion(f32[65536]{0:T(1024)S(1)} %bitcast.78, s32[256]{0:T(256)S(1)} %bitcast.117, f32[256]{0:T(256)S(1)} %bitcast.122), kind=kCustom, calls=%fused_computation.1 | custom fusion | flops 256 | bytes 4096 | tf_op jit(solution)/shard_map/scatter-add | solution.py:71
  78.9 2.3 %collective-permute-start.14 = (f32[1,4,32,128]{3,2,1,0:T(8,128)}, f32[1,4,32,128]{3,2,1,0:T(8,128)S(1)}, u32[]{:S(2)}, u32[]{:S(2)}) collective-permute-start(f32[1,4,32,128]{3,2,1,0:T(8,128)} %get-tuple-element.71), channel_id=1, source_target_pairs={{4,0},{8,4},{12,8},{5,1},{9,5},{13,9},{6,2},{10,6},{14,10},{7,3},{... | collective-permute-start | bytes 196616 | tf_op jit(solution)/shard_map/ppermute | solution.py:18
  81.3 3.7 %collective-permute-start.15 = (f32[1,4,32,128]{3,2,1,0:T(8,128)S(1)}, f32[1,4,32,128]{3,2,1,0:T(8,128)S(1)}, u32[]{:S(2)}, u32[]{:S(2)}) collective-permute-start(f32[1,4,32,128]{3,2,1,0:T(8,128)S(1)} %get-tuple-element.70), channel_id=1, source_target_pairs={{0,4},{4,8},{8,12},{1,5},{5,9},{9,13},{2,6},{6,10},{10,14},{3,7},{... | collective-permute-start | bytes 196616 | tf_op jit(solution)/shard_map/ppermute | solution.py:17
  93.5 2.4 %collective-permute-start.16 = (f32[1,4,32,128]{3,2,1,0:T(8,128)S(1)}, f32[1,4,32,128]{3,2,1,0:T(8,128)S(1)}, u32[]{:S(2)}, u32[]{:S(2)}) collective-permute-start(f32[1,4,32,128]{3,2,1,0:T(8,128)S(1)} %get-tuple-element.69), channel_id=1, source_target_pairs={{4,0},{8,4},{12,8},{5,1},{9,5},{13,9},{6,2},{10,6},{14,10},{7,3},{... | collective-permute-start | bytes 196616 | tf_op jit(solution)/shard_map/ppermute | solution.py:18
  95.9 3.5 %collective-permute-start.17 = (f32[1,4,32,128]{3,2,1,0:T(8,128)S(1)}, f32[1,4,32,128]{3,2,1,0:T(8,128)S(1)}, u32[]{:S(2)}, u32[]{:S(2)}) collective-permute-start(f32[1,4,32,128]{3,2,1,0:T(8,128)S(1)} %get-tuple-element.68), channel_id=1, source_target_pairs={{0,4},{4,8},{8,12},{1,5},{5,9},{9,13},{2,6},{6,10},{10,14},{3,7},{... | collective-permute-start | bytes 196616 | tf_op jit(solution)/shard_map/ppermute | solution.py:17
  100.0 2.4 %collective-permute-start.10 = (f32[1,4,32,128]{3,2,1,0:T(8,128)}, f32[1,4,32,128]{3,2,1,0:T(8,128)}, u32[]{:S(2)}, u32[]{:S(2)}) collective-permute-start(f32[1,4,32,128]{3,2,1,0:T(8,128)} %get-tuple-element.63), channel_id=1, source_target_pairs={{4,0},{8,4},{12,8},{5,1},{9,5},{13,9},{6,2},{10,6},{14,10},{7,3},{... | collective-permute-start | bytes 196616 | tf_op jit(solution)/shard_map/ppermute | solution.py:18
  102.4 4.1 %collective-permute-start.11 = (f32[1,4,32,128]{3,2,1,0:T(8,128)}, f32[1,4,32,128]{3,2,1,0:T(8,128)}, u32[]{:S(2)}, u32[]{:S(2)}) collective-permute-start(f32[1,4,32,128]{3,2,1,0:T(8,128)} %get-tuple-element.62), channel_id=1, source_target_pairs={{0,4},{4,8},{8,12},{1,5},{5,9},{9,13},{2,6},{6,10},{10,14},{3,7},{... | collective-permute-start | bytes 196616 | tf_op jit(solution)/shard_map/ppermute | solution.py:17
  111.3 2.1 %fusion.21 = (f32[1,16,32,128]{3,2,1,0:T(8,128)S(1)}, f32[1,16,32,128]{3,2,1,0:T(8,128)S(1)}) fusion(bf16[16,32,128]{2,1,0:T(8,128)(2,1)S(1)} %all_gather.6, f32[1,16,32,128]{3,2,1,0:T(8,128)S(1)} %bitcast.93, f32[1,16,32,128]{3,2,1,0:T(8,128)S(1)} %bitcast.104, f32[1,16,32,128]{3,2,1,0:T(8,128)S(1)} %get-tuple-element.61, ...), kind=kLoop, calls=%fused_computation.160 | loop fusion | flops 5898240 | bytes 6291456 | tf_op jit(solution)/shard_map/add | solution.py:111
  119.7 15.3 %reduce-scatter.2.cloned.1.call-done = f32[16,8,128]{2,1,0:T(8,128)} async-done(((f32[16,32,128]{2,1,0:T(8,128)}), f32[16,8,128]{2,1,0:T(8,128)}) %reduce-scatter.2.cloned.1.call-update) | async-done | bytes 65552 | tf_op jit(solution)/shard_map/reduce_scatter | solution.py:142
  (94 shorter events, 31.8 us)
Async XLA Ops:
  7.2 6.9 %copy-start.4 = (bf16[16,8,128]{2,1,0:T(8,128)(2,1)S(1)}, bf16[16,8,128]{2,1,0:T(8,128)(2,1)}, u32[]{:S(2)}) copy-start(bf16[16,8,128]{2,1,0:T(8,128)(2,1)} %param.20) | copy-start | bytes 98308
  7.2 127.8 %reduce-scatter.2.cloned.1.call-start = ((), (), s32[]{:S(2)}) async-start(), calls=%async_computation.1 | async-start | bytes 327680 | tf_op jit(solution)/shard_map/reduce_scatter | solution.py:142
  8.0 33.6 %collective-permute-start.4 = (f32[1,4,32,128]{3,2,1,0:T(8,128)S(1)}, f32[1,4,32,128]{3,2,1,0:T(8,128)S(1)}, u32[]{:S(2)}, u32[]{:S(2)}) collective-permute-start(f32[1,4,32,128]{3,2,1,0:T(8,128)S(1)} %get-tuple-element.79), channel_id=1, source_target_pairs={{4,0},{8,4},{12,8},{5,1},{9,5},{13,9},{6,2},{10,6},{14,10},{7,3},{... | collective-permute-start | bytes 196616 | tf_op jit(solution)/shard_map/ppermute | solution.py:18
  10.4 15.1 %copy-start.1 = (bf16[1,16,32,128]{3,2,1,0:T(8,128)(2,1)S(1)}, bf16[1,16,32,128]{3,2,1,0:T(8,128)(2,1)}, u32[]{:S(2)}) copy-start(bf16[1,16,32,128]{3,2,1,0:T(8,128)(2,1)} %param.23) | copy-start | bytes 393220
  10.4 31.3 %collective-permute-start.5 = (f32[1,4,32,128]{3,2,1,0:T(8,128)S(1)}, f32[1,4,32,128]{3,2,1,0:T(8,128)S(1)}, u32[]{:S(2)}, u32[]{:S(2)}) collective-permute-start(f32[1,4,32,128]{3,2,1,0:T(8,128)S(1)} %get-tuple-element.78), channel_id=1, source_target_pairs={{0,4},{4,8},{8,12},{1,5},{5,9},{9,13},{2,6},{6,10},{10,14},{3,7},{... | collective-permute-start | bytes 196616 | tf_op jit(solution)/shard_map/ppermute | solution.py:17
  19.5 18.6 %collective-permute-start.2 = (bf16[4,32,128]{2,1,0:T(8,128)(2,1)S(1)}, bf16[4,32,128]{2,1,0:T(8,128)(2,1)S(1)}, u32[]{:S(2)}, u32[]{:S(2)}) collective-permute-start(bf16[4,32,128]{2,1,0:T(8,128)(2,1)S(1)} %get-tuple-element.76), channel_id=1, source_target_pairs={{0,4},{4,8},{8,12},{1,5},{5,9},{9,13},{2,6},{6,10},{10,14},{3,7},{... | collective-permute-start | bytes 98312 | tf_op jit(solution)/shard_map/ppermute | solution.py:17
  21.4 7.1 %copy-start = (bf16[1,16,32,128]{3,2,1,0:T(8,128)(2,1)S(1)}, bf16[1,16,32,128]{3,2,1,0:T(8,128)(2,1)}, u32[]{:S(2)}) copy-start(bf16[1,16,32,128]{3,2,1,0:T(8,128)(2,1)} %param.21) | copy-start | bytes 393220
  21.4 20.1 %collective-permute-start.3 = (bf16[4,32,128]{2,1,0:T(8,128)(2,1)S(1)}, bf16[4,32,128]{2,1,0:T(8,128)(2,1)S(1)}, u32[]{:S(2)}, u32[]{:S(2)}) collective-permute-start(bf16[4,32,128]{2,1,0:T(8,128)(2,1)S(1)} %get-tuple-element.77), channel_id=1, source_target_pairs={{4,0},{8,4},{12,8},{5,1},{9,5},{13,9},{6,2},{10,6},{14,10},{7,3},{... | collective-permute-start | bytes 98312 | tf_op jit(solution)/shard_map/ppermute | solution.py:18
  25.5 28.8 %collective-permute-start = (f32[1,4,32,128]{3,2,1,0:T(8,128)S(1)}, f32[1,4,32,128]{3,2,1,0:T(8,128)S(1)}, u32[]{:S(2)}, u32[]{:S(2)}) collective-permute-start(f32[1,4,32,128]{3,2,1,0:T(8,128)S(1)} %get-tuple-element.75), channel_id=1, source_target_pairs={{4,0},{8,4},{12,8},{5,1},{9,5},{13,9},{6,2},{10,6},{14,10},{7,3},{... | collective-permute-start | bytes 196616 | tf_op jit(solution)/shard_map/ppermute | solution.py:18
  28.6 4.0 %copy-start.5 = (bf16[16,8,128]{2,1,0:T(8,128)(2,1)S(1)}, bf16[16,8,128]{2,1,0:T(8,128)(2,1)}, u32[]{:S(2)}) copy-start(bf16[16,8,128]{2,1,0:T(8,128)(2,1)} %param.19) | copy-start | bytes 98308
  38.1 16.2 %collective-permute-start.1 = (f32[1,4,32,128]{3,2,1,0:T(8,128)S(1)}, f32[1,4,32,128]{3,2,1,0:T(8,128)S(1)}, u32[]{:S(2)}, u32[]{:S(2)}) collective-permute-start(f32[1,4,32,128]{3,2,1,0:T(8,128)S(1)} %get-tuple-element.74), channel_id=1, source_target_pairs={{0,4},{4,8},{8,12},{1,5},{5,9},{9,13},{2,6},{6,10},{10,14},{3,7},{... | collective-permute-start | bytes 196616 | tf_op jit(solution)/shard_map/ppermute | solution.py:17
  48.3 15.5 %collective-permute-start.6 = (f32[1,4,32,128]{3,2,1,0:T(8,128)S(1)}, f32[1,4,32,128]{3,2,1,0:T(8,128)S(1)}, u32[]{:S(2)}, u32[]{:S(2)}) collective-permute-start(f32[1,4,32,128]{3,2,1,0:T(8,128)S(1)} %get-tuple-element.67), channel_id=1, source_target_pairs={{4,0},{8,4},{12,8},{5,1},{9,5},{13,9},{6,2},{10,6},{14,10},{7,3},{... | collective-permute-start | bytes 196616 | tf_op jit(solution)/shard_map/ppermute | solution.py:18
  50.7 4.0 %copy-start.3 = (bf16[1,16,32,128]{3,2,1,0:T(8,128)(2,1)S(1)}, bf16[1,16,32,128]{3,2,1,0:T(8,128)(2,1)}, u32[]{:S(2)}) copy-start(bf16[1,16,32,128]{3,2,1,0:T(8,128)(2,1)} %param.24) | copy-start | bytes 393220
  50.7 13.1 %collective-permute-start.7 = (f32[1,4,32,128]{3,2,1,0:T(8,128)S(1)}, f32[1,4,32,128]{3,2,1,0:T(8,128)S(1)}, u32[]{:S(2)}, u32[]{:S(2)}) collective-permute-start(f32[1,4,32,128]{3,2,1,0:T(8,128)S(1)} %get-tuple-element.66), channel_id=1, source_target_pairs={{0,4},{4,8},{8,12},{1,5},{5,9},{9,13},{2,6},{6,10},{10,14},{3,7},{... | collective-permute-start | bytes 196616 | tf_op jit(solution)/shard_map/ppermute | solution.py:17
  57.9 16.7 %collective-permute-start.12 = (f32[1,4,32,128]{3,2,1,0:T(8,128)S(1)}, f32[1,4,32,128]{3,2,1,0:T(8,128)S(1)}, u32[]{:S(2)}, u32[]{:S(2)}) collective-permute-start(f32[1,4,32,128]{3,2,1,0:T(8,128)S(1)} %get-tuple-element.73), channel_id=1, source_target_pairs={{4,0},{8,4},{12,8},{5,1},{9,5},{13,9},{6,2},{10,6},{14,10},{7,3},{... | collective-permute-start | bytes 196616 | tf_op jit(solution)/shard_map/ppermute | solution.py:18
  60.3 14.3 %collective-permute-start.13 = (f32[1,4,32,128]{3,2,1,0:T(8,128)S(1)}, f32[1,4,32,128]{3,2,1,0:T(8,128)S(1)}, u32[]{:S(2)}, u32[]{:S(2)}) collective-permute-start(f32[1,4,32,128]{3,2,1,0:T(8,128)S(1)} %get-tuple-element.72), channel_id=1, source_target_pairs={{0,4},{4,8},{8,12},{1,5},{5,9},{9,13},{2,6},{6,10},{10,14},{3,7},{... | collective-permute-start | bytes 196616 | tf_op jit(solution)/shard_map/ppermute | solution.py:17
  68.8 16.1 %collective-permute-start.8 = (f32[1,4,32,128]{3,2,1,0:T(8,128)S(1)}, f32[1,4,32,128]{3,2,1,0:T(8,128)S(1)}, u32[]{:S(2)}, u32[]{:S(2)}) collective-permute-start(f32[1,4,32,128]{3,2,1,0:T(8,128)S(1)} %get-tuple-element.65), channel_id=1, source_target_pairs={{4,0},{8,4},{12,8},{5,1},{9,5},{13,9},{6,2},{10,6},{14,10},{7,3},{... | collective-permute-start | bytes 196616 | tf_op jit(solution)/shard_map/ppermute | solution.py:18
  71.1 13.8 %collective-permute-start.9 = (f32[1,4,32,128]{3,2,1,0:T(8,128)S(1)}, f32[1,4,32,128]{3,2,1,0:T(8,128)S(1)}, u32[]{:S(2)}, u32[]{:S(2)}) collective-permute-start(f32[1,4,32,128]{3,2,1,0:T(8,128)S(1)} %get-tuple-element.64), channel_id=1, source_target_pairs={{0,4},{4,8},{8,12},{1,5},{5,9},{9,13},{2,6},{6,10},{10,14},{3,7},{... | collective-permute-start | bytes 196616 | tf_op jit(solution)/shard_map/ppermute | solution.py:17
  78.9 11.0 %collective-permute-start.14 = (f32[1,4,32,128]{3,2,1,0:T(8,128)}, f32[1,4,32,128]{3,2,1,0:T(8,128)S(1)}, u32[]{:S(2)}, u32[]{:S(2)}) collective-permute-start(f32[1,4,32,128]{3,2,1,0:T(8,128)} %get-tuple-element.71), channel_id=1, source_target_pairs={{4,0},{8,4},{12,8},{5,1},{9,5},{13,9},{6,2},{10,6},{14,10},{7,3},{... | collective-permute-start | bytes 196616 | tf_op jit(solution)/shard_map/ppermute | solution.py:18
  81.3 8.6 %collective-permute-start.15 = (f32[1,4,32,128]{3,2,1,0:T(8,128)S(1)}, f32[1,4,32,128]{3,2,1,0:T(8,128)S(1)}, u32[]{:S(2)}, u32[]{:S(2)}) collective-permute-start(f32[1,4,32,128]{3,2,1,0:T(8,128)S(1)} %get-tuple-element.70), channel_id=1, source_target_pairs={{0,4},{4,8},{8,12},{1,5},{5,9},{9,13},{2,6},{6,10},{10,14},{3,7},{... | collective-permute-start | bytes 196616 | tf_op jit(solution)/shard_map/ppermute | solution.py:17
  93.5 13.0 %collective-permute-start.16 = (f32[1,4,32,128]{3,2,1,0:T(8,128)S(1)}, f32[1,4,32,128]{3,2,1,0:T(8,128)S(1)}, u32[]{:S(2)}, u32[]{:S(2)}) collective-permute-start(f32[1,4,32,128]{3,2,1,0:T(8,128)S(1)} %get-tuple-element.69), channel_id=1, source_target_pairs={{4,0},{8,4},{12,8},{5,1},{9,5},{13,9},{6,2},{10,6},{14,10},{7,3},{... | collective-permute-start | bytes 196616 | tf_op jit(solution)/shard_map/ppermute | solution.py:18
  95.9 10.6 %collective-permute-start.17 = (f32[1,4,32,128]{3,2,1,0:T(8,128)S(1)}, f32[1,4,32,128]{3,2,1,0:T(8,128)S(1)}, u32[]{:S(2)}, u32[]{:S(2)}) collective-permute-start(f32[1,4,32,128]{3,2,1,0:T(8,128)S(1)} %get-tuple-element.68), channel_id=1, source_target_pairs={{0,4},{4,8},{8,12},{1,5},{5,9},{9,13},{2,6},{6,10},{10,14},{3,7},{... | collective-permute-start | bytes 196616 | tf_op jit(solution)/shard_map/ppermute | solution.py:17
  100.0 10.1 %collective-permute-start.10 = (f32[1,4,32,128]{3,2,1,0:T(8,128)}, f32[1,4,32,128]{3,2,1,0:T(8,128)}, u32[]{:S(2)}, u32[]{:S(2)}) collective-permute-start(f32[1,4,32,128]{3,2,1,0:T(8,128)} %get-tuple-element.63), channel_id=1, source_target_pairs={{4,0},{8,4},{12,8},{5,1},{9,5},{13,9},{6,2},{10,6},{14,10},{7,3},{... | collective-permute-start | bytes 196616 | tf_op jit(solution)/shard_map/ppermute | solution.py:18
  102.4 7.7 %collective-permute-start.11 = (f32[1,4,32,128]{3,2,1,0:T(8,128)}, f32[1,4,32,128]{3,2,1,0:T(8,128)}, u32[]{:S(2)}, u32[]{:S(2)}) collective-permute-start(f32[1,4,32,128]{3,2,1,0:T(8,128)} %get-tuple-element.62), channel_id=1, source_target_pairs={{0,4},{4,8},{8,12},{1,5},{5,9},{9,13},{2,6},{6,10},{10,14},{3,7},{... | collective-permute-start | bytes 196616 | tf_op jit(solution)/shard_map/ppermute | solution.py:17
  (5 other events, 3.6 us)
Sparse Core Ops, SparseCore 0:
  114.6 20.4 reduce-scatter.1
where the time goes:
time: 145 us; the launch traced here: 142 us
  starting transfers between devices  53.8 us (37%)
  other arithmetic  33.2 us (23%)
  between operations  23.6 us (16%)
  waiting for transfers between devices  15.4 us (11%)
  blocking collectives  10.9 us (8%)
  local copies, waits for them, and re-layouts  5.13 us (4%)
    ppermute x9, starting transfers between devices, extended_2(): before = lax.ppermute(last, axis, up)  30.8 us
    ppermute x9, starting transfers between devices, extended_2(): after = lax.ppermute(initial, axis, down)  22.9 us
    reduce_scatter x1, waiting for transfers between devices, local(): lax.psum_scatter(local_term, 'shot', scatter_dimension=1, tiled=True)  15.3 us
    scatter-add x4, other arithmetic, inject(): flat_field = flat_field.at[slot_rows, local_cell].add(values, mode='drop')  8.28 us
    add x4, other arithmetic, local(): forward_next = 2.0 * current - previous + courant_sq * applied  6.73 us
    all_gather x1, blocking collectives, local(): lax.all_gather(density, 'shot', axis=1, tiled=True)  5.45 us
    all_gather x1, blocking collectives, local(): lax.all_gather(velocity, 'shot', axis=1, tiled=True)  5.43 us
    add x4, other arithmetic, inject(): flat_field = flat_field.at[slot_rows, local_cell].add(values, mode='drop')  5.03 us
  transfers between devices with their start and end apart: 19, of which 1 were waited for; matrix products, arithmetic and copies ran while one was open for 20% of the time, Pallas kernels for 0%

commit v1 on v0

v1 whole, which is shorter than its diff:
```python
import jax
import jax.numpy as jnp
from jax import lax
from jax.experimental import pallas as pl
from jax.experimental.pallas import tpu as pltpu
from jax.sharding import PartitionSpec as P

FIRST = (672.0, -168.0, 32.0, -3.0)
SECOND = (8064.0, -1008.0, 128.0, -9.0)
CENTRE = -3.0 * 14350.0
SCALE = 5040.0
STEPS = 4
HALO = 4
PAD = 8
VMEM_BYTES = 24 * 1024 * 1024


def vmem():
    return pl.BlockSpec(memory_space=pltpu.VMEM)


def smem():
    return pl.BlockSpec(memory_space=pltpu.SMEM)


def two_terms(values):
    high = values.astype(jnp.bfloat16)
    low = (values - high.astype(jnp.float32)).astype(jnp.bfloat16)
    return high, low


def is_active(aperture_ref, tile):
    found = aperture_ref[0, 0] == tile
    for slot in range(1, aperture_ref.shape[1]):
        found = found | (aperture_ref[0, slot] == tile)
    return found & (tile >= 0)


def layout(aperture_ref, cx):
    tiles = lax.axis_size("tile")
    tile = lax.axis_index("tile")
    even = lax.rem(tile, 2) == 0
    left = is_active(aperture_ref, tile - 1) & (tile > 0)
    right = is_active(aperture_ref, tile + 1) & (tile < tiles - 1)
    own = is_active(aperture_ref, tile)
    a_tile = jnp.where(even, tile + 1, tile - 1)
    b_tile = jnp.where(even, tile - 1, tile + 1)
    a_at = jnp.where(even, 2 * cx, 0)
    b_at = jnp.where(even, 0, 2 * cx)
    a_here = (a_tile >= 0) & (a_tile < tiles)
    b_here = (b_tile >= 0) & (b_tile < tiles)
    a_on = jnp.where(even, right, left)
    b_on = jnp.where(even, left, right)
    return tile, own, left, right, (a_at, a_here, a_on), (b_at, b_here, b_on)


def bounds(step, left, right, cx):
    reach = (STEPS - 1 - step) * HALO
    low = jnp.where(left, cx - reach, cx) // HALO
    high = jnp.where(right, 2 * cx + reach, 2 * cx) // HALO
    return low, high


def setup_kernel(cx, cells_ref, traces_ref, weights_ref, add_ref):
    ny, nz = 32, 128
    rows = lax.broadcasted_iota(jnp.int32, (2 * nz, 2 * nz), 0)
    cols = lax.broadcasted_iota(jnp.int32, (2 * nz, 2 * nz), 1)
    ahead = lax.rem(rows, nz) - lax.rem(cols, nz)
    first = jnp.zeros((2 * nz, 2 * nz), jnp.float32)
    second = jnp.zeros((2 * nz, 2 * nz), jnp.float32)
    for k in range(1, 5):
        first = jnp.where(ahead == k, FIRST[k - 1], jnp.where(ahead == -k, -FIRST[k - 1], first))
        second = jnp.where((ahead == k) | (ahead == -k), SECOND[k - 1], second)
    weights_ref[...] = jnp.where(cols < nz, first, second).astype(jnp.bfloat16)

    tile = lax.axis_index("tile")
    count = cells_ref.shape[1]
    cells = cells_ref[...]
    at_row = cells // nz - (tile - 1) * (cx * ny)
    at_z = lax.rem(cells, nz)
    depth = lax.broadcasted_iota(jnp.int32, (nz, count), 0)
    depth_hot = jnp.where(depth == at_z, 1.0, 0.0).astype(jnp.bfloat16)
    depth_hot = jnp.concatenate([depth_hot, depth_hot], axis=1)
    block = HALO * ny
    row = lax.broadcasted_iota(jnp.int32, (block, count), 0)
    base = 0
    for step in range(STEPS):
        reach = (STEPS - 1 - step) * HALO
        layers = cx + 2 * reach
        trace = traces_ref[0, pl.ds(STEPS - 1 - step, 1), :]
        high = trace.astype(jnp.bfloat16).astype(jnp.float32)
        low = trace - high

        def body(c, carry, base=base, reach=reach, high=high, low=low):
            hot = at_row == row + (cx - reach + c * HALO) * ny
            spread = jnp.concatenate([jnp.where(hot, high, 0.0), jnp.where(hot, low, 0.0)], axis=1).astype(jnp.bfloat16)
            value = lax.dot_general(spread, depth_hot, (((1,), (1,)), ((), ())), preferred_element_type=jnp.float32)
            add_ref[pl.ds(base + c * HALO, HALO)] = value.reshape(HALO, ny, nz)
            return carry

        lax.fori_loop(0, layers // HALO, body, 0)
        base += layers


def differences(buf, i0, weights, ny):
    nz = buf.shape[2]
    middle = buf[pl.ds(i0, HALO), PAD : PAD + ny, :]
    high, low = two_terms(middle.reshape(HALO * ny, nz))
    along_z = jnp.dot(jnp.concatenate([high, low], axis=1), weights, preferred_element_type=jnp.float32)
    along_z = along_z.reshape(HALO, ny, 2 * nz)
    out = []
    for j in range(HALO):
        sums = along_z[j, :, nz:]
        firsts = []
        for axis in range(2):
            first = None
            for k in range(1, 5):
                if axis == 0:
                    plus = buf[i0 + j + k, PAD : PAD + ny, :]
                    minus = buf[i0 + j - k, PAD : PAD + ny, :]
                else:
                    plus = buf[i0 + j, PAD + k : PAD + k + ny, :]
                    minus = buf[i0 + j, PAD - k : PAD - k + ny, :]
                sums = sums + SECOND[k - 1] * (plus + minus)
                term = FIRST[k - 1] * (plus - minus)
                first = term if first is None else first + term
            firsts.append(first)
        firsts.append(along_z[j, :, :nz])
        out.append((middle[j], sums, firsts))
    return out


def march(step, cur, prev, slopes_ref, courant_ref, weights, span, cx, ny, use):
    def body(c, carry):
        i0 = c * HALO
        for j, (centre, sums, firsts) in enumerate(differences(cur, i0, weights, ny)):
            applied = CENTRE * centre + sums
            for axis in range(3):
                applied = applied - slopes_ref[axis, i0 + j] * firsts[axis]
            updated = 2.0 * centre - prev[i0 + j, PAD : PAD + ny, :] + courant_ref[i0 + j] * applied
            updated = use(c, j, applied, updated)
            prev[i0 + j, PAD : PAD + ny, :] = updated
        return carry

    lax.fori_loop(span[0], span[1], body, 0)


def fill(buf, at, rows_ref, first_row, cx, ny, nz, keep):
    part = rows_ref[pl.ds(first_row, cx * ny), :].astype(jnp.float32)
    if keep is not None:
        part = jnp.where(keep, part, 0.0)
    buf[pl.ds(at, cx), PAD : PAD + ny, :] = part.reshape(cx, ny, nz)


def fill_fields(now, before, own_now, own_before, from_a, from_b, side_a, side_b, cx, ny, nz):
    zero = jnp.zeros((3 * cx, PAD, nz), jnp.float32)
    for buf in (now, before):
        buf[:, 0:PAD, :] = zero
        buf[:, PAD + ny : 2 * PAD + ny, :] = zero
    fill(now, cx, own_now, 0, cx, ny, nz, None)
    fill(before, cx, own_before, 0, cx, ny, nz, None)
    for ref, (at, here, on) in ((from_a, side_a), (from_b, side_b)):
        fill(now, at, ref, 0, cx, ny, nz, here)
        fill(before, at, ref, cx * ny, cx, ny, nz, on)


def clear_sides(buf, left, right, cx, ny, nz):
    zero = jnp.zeros((HALO, ny, nz), jnp.float32)

    @pl.when(jnp.logical_not(left))
    def _():
        buf[cx - HALO : cx, PAD : PAD + ny, :] = zero

    @pl.when(jnp.logical_not(right))
    def _():
        buf[2 * cx : 2 * cx + HALO, PAD : PAD + ny, :] = zero


def forward_kernel(
    cx, ny, nz, order, aperture_ref, source_ref, wavelet_ref, *refs
):
    model_refs = refs[: len(order)]
    weights_ref, own_now, own_before, from_a, from_b = refs[len(order) : len(order) + 5]
    slopes_ref, courant_ref, stored_ref, end_ref, gain_ref, log_buf, now, before = refs[len(order) + 5 :]
    tile, own, left, right, side_a, side_b = layout(aperture_ref, cx)
    shot = lax.axis_index("shot")
    sides = ((cx, None), (side_a[0], side_a[1]), (side_b[0], side_b[1]))
    block_rows = ny // len(order)
    size = cx * block_rows

    @pl.when(jnp.logical_not(own))
    def _():
        end_ref[...] = jnp.zeros_like(end_ref)

    @pl.when(own)
    def _():
        zero = jnp.zeros((3 * cx, PAD, nz), jnp.float32)
        log_buf[:, 0:PAD, :] = zero
        log_buf[:, PAD + ny : 2 * PAD + ny, :] = zero
        for ref, mask in zip(model_refs, order):
            y0 = pl.multiple_of((shot ^ mask) * block_rows, block_rows)
            for place, (at, here) in enumerate(sides):
                base = place * 2 * size
                speed = ref[pl.ds(base, size), :].astype(jnp.float32)
                courant = (speed * speed) * (1.0 / SCALE)
                courant_ref[pl.ds(at, cx), pl.ds(y0, block_rows), :] = courant.reshape(cx, block_rows, nz)
                if here is None:
                    gain = speed * (2.0 / SCALE)
                    gain_ref[:, pl.ds(y0, block_rows), :] = gain.reshape(cx, block_rows, nz)
                logs = jnp.log(ref[pl.ds(base + size, size), :].astype(jnp.float32))
                if here is not None:
                    logs = jnp.where(here, logs, 0.0)
                log_buf[pl.ds(at, cx), pl.ds(PAD + y0, block_rows), :] = logs.reshape(cx, block_rows, nz)
        fill_fields(now, before, own_now, own_before, from_a, from_b, side_a, side_b, cx, ny, nz)
        weights = weights_ref[...]

        def slope_body(c, carry):
            i0 = c * HALO
            for j, (centre, sums, firsts) in enumerate(differences(log_buf, i0, weights, ny)):
                for axis in range(3):
                    slopes_ref[axis, i0 + j] = firsts[axis] * (1.0 / 140.0)
            return carry

        span = bounds(0, left, right, cx)
        lax.fori_loop(span[0], span[1], slope_body, 0)

        cell = source_ref[0]
        layer = cell // (ny * nz) - (tile - 1) * cx
        row = lax.rem(cell // nz, ny)
        depth = lax.rem(cell, nz)
        lanes = lax.broadcasted_iota(jnp.int32, (1, nz), 1)
        bufs = (now, before)
        for step in range(STEPS):
            cur, prev = bufs[step % 2], bufs[(step + 1) % 2]
            span = bounds(step, left, right, cx)

            def use(c, j, applied, updated, step=step):
                inner = (c >= cx // HALO) & (c < 2 * cx // HALO)
                at = jnp.where(inner, c * HALO - cx, cx)
                stored_ref[step, at + j] = applied
                return updated

            march(step, cur, prev, slopes_ref, courant_ref, weights, span, cx, ny, use)
            inside = (layer >= span[0] * HALO) & (layer < span[1] * HALO)
            value = wavelet_ref[0, step]

            @pl.when(inside)
            def _(prev=prev, value=value):
                old = prev[layer, pl.ds(PAD + row, 1), :]
                prev[layer, pl.ds(PAD + row, 1), :] = old + jnp.where(lanes == depth, value, 0.0)

            if step == 0:
                clear_sides(cur, left, right, cx, ny, nz)
        last = bufs[STEPS % 2]
        end_ref[...] = last[cx : 2 * cx, PAD : PAD + ny, :].reshape(cx * ny, nz).astype(jnp.bfloat16)


def adjoint_kernel(
    cx, ny, nz, order, aperture_ref, gain_ref, weights_ref, slopes_ref, courant_ref, stored_ref, add_ref, own_now, own_before,
    from_a, from_b, sums_ref, start_ref, now, before, image,
):
    tile, own, left, right, side_a, side_b = layout(aperture_ref, cx)
    shot = lax.axis_index("shot")
    block_rows = ny // len(order)

    @pl.when(jnp.logical_not(own))
    def _():
        start_ref[...] = jnp.zeros_like(start_ref)
        sums_ref[...] = jnp.zeros_like(sums_ref)

    @pl.when(own)
    def _():
        fill_fields(now, before, own_now, own_before, from_a, from_b, side_a, side_b, cx, ny, nz)
        weights = weights_ref[...]
        bufs = (now, before)
        base = 0
        for step in range(STEPS):
            cur, prev = bufs[step % 2], bufs[(step + 1) % 2]
            span = bounds(step, left, right, cx)
            reach = (STEPS - 1 - step) * HALO

            def use(c, j, applied, updated, step=step, base=base, reach=reach):
                updated = updated + add_ref[base + reach - cx + c * HALO + j]
                inner = (c >= cx // HALO) & (c < 2 * cx // HALO)
                at = jnp.where(inner, c * HALO - cx, cx)
                term = updated * stored_ref[STEPS - 1 - step, at + j]
                image[at + j] = term if step == 0 else image[at + j] + term
                return updated

            march(step, cur, prev, slopes_ref, courant_ref, weights, span, cx, ny, use)
            if step == 0:
                clear_sides(cur, left, right, cx, ny, nz)
            base += cx + 2 * reach
        last = bufs[STEPS % 2]
        start_ref[...] = last[cx : 2 * cx, PAD : PAD + ny, :].reshape(cx * ny, nz).astype(jnp.bfloat16)
        for place, mask in enumerate(order):
            y0 = pl.multiple_of((shot ^ mask) * block_rows, block_rows)
            gain = gain_ref[:, pl.ds(y0, block_rows), :]
            sums_ref[place] = (gain * image[0:cx, pl.ds(y0, block_rows), :]).reshape(cx * block_rows, nz)


def pairs(axis_sizes, kind):
    tiles, shots = axis_sizes
    found = []
    for tile in range(tiles):
        other = tile ^ 1 if kind == "a" else ((tile + 1) ^ 1) - 1
        for shot in range(shots):
            here = tile * shots + shot
            if 0 <= other < tiles:
                found.append((here, other * shots + shot))
            elif shots % 2 == 0:
                found.append((here, tile * shots + (shot ^ 1)))
    return found


def local(
    velocity, density, wave_now, wave_before, adjoint_end, adjoint_after, source_cell, source_wave, receiver_cell, residual_traces,
    aperture,
):
    cx, _, nz = velocity.shape
    ny = wave_now.shape[2]
    shots = lax.axis_size("shot")
    tiles = lax.axis_size("tile")
    rows = cx * ny
    params = pltpu.CompilerParams(vmem_limit_bytes=VMEM_BYTES)

    def swap(x, kind):
        return lax.ppermute(x, ("tile", "shot"), pairs((tiles, shots), kind))

    def cross(x, mask):
        return lax.ppermute(x, "shot", [(i, i ^ mask) for i in range(shots)])

    model = jnp.concatenate([velocity.reshape(-1, nz), density.reshape(-1, nz)], axis=0)
    model_a, model_b = swap(model, "a"), swap(model, "b")
    forward = jnp.concatenate([wave_now.reshape(rows, nz), wave_before.reshape(rows, nz)], axis=0)
    forward_a, forward_b = swap(forward, "a"), swap(forward, "b")
    adjoint = jnp.concatenate([adjoint_end.reshape(rows, nz), adjoint_after.reshape(rows, nz)], axis=0)
    adjoint_a, adjoint_b = swap(adjoint, "a"), swap(adjoint, "b")

    held = [(0, jnp.concatenate([model, model_a, model_b], axis=0))]
    mask = shots // 2
    while mask:
        if len(held) > 1:
            moved = cross(jnp.stack([block for _, block in held]), mask)
            held = held + [(m ^ mask, moved[i]) for i, (m, _) in enumerate(held)]
        else:
            held = held + [(mask, cross(held[0][1], mask))]
        mask //= 2

    added_layers = sum(cx + 2 * (STEPS - 1 - step) * HALO for step in range(STEPS))
    weights, added = pl.pallas_call(
        lambda *refs: setup_kernel(cx, *refs),
        out_shape=(
            jax.ShapeDtypeStruct((2 * nz, 2 * nz), jnp.bfloat16),
            jax.ShapeDtypeStruct((added_layers, ny, nz), jnp.float32),
        ),
        in_specs=[vmem()] * 2,
        out_specs=(vmem(), vmem()),
        compiler_params=params,
        name="receivers",
    )(receiver_cell, residual_traces)

    order = tuple(m for m, _ in held)
    field = pltpu.VMEM((3 * cx, 2 * PAD + ny, nz), jnp.float32)
    slopes, courant, stored, wave_end, gain = pl.pallas_call(
        lambda *refs: forward_kernel(cx, ny, nz, order, *refs),
        out_shape=(
            jax.ShapeDtypeStruct((3, 3 * cx, ny, nz), jnp.float32),
            jax.ShapeDtypeStruct((3 * cx, ny, nz), jnp.float32),
            jax.ShapeDtypeStruct((STEPS, cx + HALO, ny, nz), jnp.float32),
            jax.ShapeDtypeStruct((rows, nz), jnp.bfloat16),
            jax.ShapeDtypeStruct((cx, ny, nz), jnp.float32),
        ),
        in_specs=[smem()] * 3 + [vmem()] * (len(order) + 5),
        out_specs=(vmem(),) * 5,
        scratch_shapes=[field, field, field],
        compiler_params=params,
        name="forward",
    )(
        aperture, source_cell, source_wave, *[block for _, block in held], weights,
        wave_now.reshape(rows, nz), wave_before.reshape(rows, nz), forward_a, forward_b,
    )

    bits = []
    mask = 1
    while mask < shots:
        bits.append(mask)
        mask *= 2
    sum_order = [0]
    for bit in reversed(bits):
        sum_order = sum_order + [m | bit for m in sum_order]
    sum_order = tuple(sum_order)
    block = cx * (ny // shots)
    sums, adjoint_start = pl.pallas_call(
        lambda *refs: adjoint_kernel(cx, ny, nz, sum_order, *refs),
        out_shape=(
            jax.ShapeDtypeStruct((shots, block, nz), jnp.float32),
            jax.ShapeDtypeStruct((rows, nz), jnp.bfloat16),
        ),
        in_specs=[smem()] + [vmem()] * 10,
        out_specs=(vmem(),) * 2,
        scratch_shapes=[field, field, pltpu.VMEM((cx + HALO, ny, nz), jnp.float32)],
        compiler_params=params,
        name="adjoint",
    )(
        aperture, gain, weights, slopes, courant, stored, added, adjoint_end.reshape(rows, nz), adjoint_after.reshape(rows, nz),
        adjoint_a, adjoint_b,
    )
    for bit in bits:
        half = sums.shape[0] // 2
        sums = sums[:half] + cross(sums[half:], bit)
    gradient = sums[0].reshape(cx, ny // shots, nz)
    return gradient, wave_end.reshape(wave_now.shape), adjoint_start.reshape(wave_now.shape)


def solution(mesh):
    stored = P(("parts", "tile"), "shot", None)
    field = P(("parts", "shot"), "tile", None, None)
    return jax.shard_map(
        local,
        mesh=mesh,
        in_specs=(
            stored, stored, field, field, field, field, P(("parts", "shot")), P(("parts", "shot"), None),
            P(("parts", "shot"), None), P(("parts", "shot"), None, None), P(("parts", "shot"), None),
        ),
        out_specs=(stored, field, field),
        check_vma=False,
    )
```

time: 145 us -> 46.3 us (0.32); the launches traced: 142 us -> 45.6 us
  starting transfers between devices: 53.8 us -> 6.38 us
  other arithmetic: 33.2 us -> 3.43 us
  between operations: 23.6 us -> 1.46 us
  Pallas kernels: 0 us -> 20.2 us
  blocking collectives: 10.9 us -> 0 us
  local copies, waits for them, and re-layouts: 5.13 us -> 0.08 us
    ppermute x18 -> x10, starting transfers between devices: 53.7 us -> 6.38 us  [the longest x6 4.06 us: swap(): return lax.ppermute(x, ('tile', 'shot'), pairs((tiles, shots), kind))]
    pallas_call x0 -> x3, Pallas kernels: none -> 20.2 us  [the longest x1 7.96 us: local(): pl.pallas_call(lambda *refs: forward_kernel(cx, ny, nz, order, *refs), ou...]
    add x12 -> x1, other arithmetic: 16.4 us -> 0.02 us  [local(): sums = sums[:half] + cross(sums[half:], bit)]
    reduce_scatter x1 -> x0, waiting for transfers between devices: 15.3 us -> none  [local(): lax.psum_scatter(local_term, 'shot', scatter_dimension=1, tiled=True)]
    ppermute x18 -> x10, waiting for transfers between devices: 0.05 us -> 14 us  [the longest x4 9.23 us: cross(): return lax.ppermute(x, 'shot', [(i, i ^ mask) for i in range(shots)])]
    all_gather x2 -> x0, blocking collectives: 10.9 us -> none  [the longest x1 5.45 us: local(): lax.all_gather(density, 'shot', axis=1, tiled=True)]
    scatter-add x4 -> x0, other arithmetic: 8.28 us -> none  [inject(): flat_field = flat_field.at[slot_rows, local_cell].add(values, mode='drop')]
    slice x11 -> x2, local copies, waits for them, and re-layouts: 2.82 us -> 0.02 us  [local(): sums = sums[:half] + cross(sums[half:], bit)]
  transfers between devices with their start and end apart: 19 -> 10, of which waited for: 1 -> 7; matrix products, arithmetic and copies ran while one was open for 20% -> 2% of each run, Pallas kernels for 0% -> 29%
where the time goes in v1:
time: 46.3 us; the launch traced here: 45.6 us
  Pallas kernels  20.2 us (44%)
  waiting for transfers between devices  14 us (30%)
  starting transfers between devices  6.38 us (14%)
  other arithmetic  3.43 us (7%)
  between operations  1.46 us (3%)
    ppermute x4, waiting for transfers between devices, cross(): return lax.ppermute(x, 'shot', [(i, i ^ mask) for i in range(shots)])  9.23 us
    pallas_call x1, Pallas kernels, local(): pl.pallas_call(lambda *refs: forward_kernel(cx, ny, nz, order, *refs), ou...  7.96 us
    pallas_call x1, Pallas kernels, local(): pl.pallas_call(lambda *refs: adjoint_kernel(cx, ny, nz, sum_order, *refs)...  6.79 us
    pallas_call x1, Pallas kernels, local(): pl.pallas_call(lambda *refs: setup_kernel(cx, *refs), out_shape=(jax.Shap...  5.47 us
    ppermute x6, waiting for transfers between devices, swap(): return lax.ppermute(x, ('tile', 'shot'), pairs((tiles, shots), kind))  4.8 us
    ppermute x6, starting transfers between devices, swap(): return lax.ppermute(x, ('tile', 'shot'), pairs((tiles, shots), kind))  4.06 us
    ppermute x4, starting transfers between devices, cross(): return lax.ppermute(x, 'shot', [(i, i ^ mask) for i in range(shots)])  2.31 us
    concatenate x1, other arithmetic, local(): jnp.concatenate([wave_now.reshape(rows, nz), wave_before.reshape(rows, nz...  0.99 us
  transfers between devices with their start and end apart: 10, of which 7 were waited for; matrix products, arithmetic and copies ran while one was open for 2% of the time, Pallas kernels for 29%

profile of v1, /device:TPU:16, one launch (start us, length us, event | category | flops | bytes accessed | tf_op | source)
XLA Modules:
  0.0 45.6 jit_solution(13965493096239122632)
XLA Ops:
  0.6 0.0 copy-start.3
  0.7 0.9 %pad_maximum_fusion.4 = bf16[256,128]{1,0:T(8,128)(2,1)S(1)} fusion(bf16[128,128]{1,0:T(8,128)(2,1)} %bitcast.26, bf16[128,128]{1,0:T(8,128)(2,1)} %bitcast.28), kind=kLoop, calls=%fused_computation.9 | loop fusion | flops 131072 | bytes 131072 | tf_op jit(solution)/shard_map/concatenate | solution.py:333
  1.6 1.6 %collective-permute-start = (bf16[256,128]{1,0:T(8,128)(2,1)S(1)}, bf16[256,128]{1,0:T(8,128)(2,1)S(1)}, u32[]{:S(2)}, u32[]{:S(2)}) collective-permute-start(bf16[256,128]{1,0:T(8,128)(2,1)S(1)} %pad_maximum_fusion.4), channel_id=1, source_target_pairs={{0,4},{1,5},{2,6},{3,7},{4,0},{5,1},{6,2},{7,3},{8,12},{9,13},{10,... | collective-permute-start | bytes 196616 | tf_op jit(solution)/shard_map/ppermute | solution.py:328
  3.2 2.7 %collective-permute-done = bf16[256,128]{1,0:T(8,128)(2,1)S(1)} collective-permute-done((bf16[256,128]{1,0:T(8,128)(2,1)S(1)}, bf16[256,128]{1,0:T(8,128)(2,1)S(1)}, u32[]{:S(2)}, u32[]{:S(2)}) %collective-permute-start) | collective-permute-done | bytes 65568 | tf_op jit(solution)/shard_map/ppermute | solution.py:328
  5.9 1.6 %collective-permute-done.1 = bf16[256,128]{1,0:T(8,128)(2,1)S(1)} collective-permute-done((bf16[256,128]{1,0:T(8,128)(2,1)S(1)}, bf16[256,128]{1,0:T(8,128)(2,1)S(1)}, u32[]{:S(2)}, u32[]{:S(2)}) %collective-permute-start.1) | collective-permute-done | bytes 65568 | tf_op jit(solution)/shard_map/ppermute | solution.py:328
  7.5 0.8 %fusion.1 = (bf16[1,768,128]{2,1,0:T(8,128)(2,1)S(1)}, bf16[768,128]{1,0:T(8,128)(2,1)S(1)}) fusion(bf16[256,128]{1,0:T(8,128)(2,1)S(1)} %collective-permute-done.1, bf16[256,128]{1,0:T(8,128)(2,1)S(1)} %collective-permute-done, bf16[128,128]{1,0:T(8,128)(2,1)} %bitcast.27, bf16[128,128]{1,0:T(8,128)(2,1)} %bitcast.29), kind=kLoop, calls=%fused_computation.10 | loop fusion | flops 786432 | bytes 589824 | tf_op jit(solution)/shard_map/stack | solution.py:344
  8.3 1.6 %collective-permute-start.2 = (bf16[768,128]{1,0:T(8,128)(2,1)S(1)}, bf16[768,128]{1,0:T(8,128)(2,1)S(1)}, u32[]{:S(2)}, u32[]{:S(2)}) collective-permute-start(bf16[768,128]{1,0:T(8,128)(2,1)S(1)} %get-tuple-element.24.refs_3_), channel_id=1, source_target_pairs={{0,2},{1,3},{2,0},{3,1},{4,6},{5,7},{6,4},{7,5},{8,10},{9,11},{10,... | collective-permute-start | bytes 589832 | tf_op jit(solution)/shard_map/ppermute | solution.py:331
  9.9 4.2 %collective-permute-done.2.refs_4_ = bf16[768,128]{1,0:T(8,128)(2,1)S(1)} collective-permute-done((bf16[768,128]{1,0:T(8,128)(2,1)S(1)}, bf16[768,128]{1,0:T(8,128)(2,1)S(1)}, u32[]{:S(2)}, u32[]{:S(2)}) %collective-permute-start.2) | collective-permute-done | bytes 196640 | tf_op jit(solution)/shard_map/ppermute | solution.py:331
  14.1 0.1 collective-permute-start.3
  14.2 1.0 %pad_maximum_fusion.1 = bf16[1024,128]{1,0:T(8,128)(2,1)S(1)} fusion(bf16[512,128]{1,0:T(8,128)(2,1)} %bitcast.24, bf16[512,128]{1,0:T(8,128)(2,1)} %bitcast.22), kind=kLoop, calls=%fused_computation.1 | loop fusion | flops 524288 | bytes 524288 | tf_op jit(solution)/shard_map/concatenate | solution.py:335
  15.1 0.1 collective-permute-start.4
  15.2 0.2 collective-permute-start.5
  15.4 2.1 %collective-permute-start.6 = (bf16[1024,128]{1,0:T(8,128)(2,1)S(1)}, bf16[1024,128]{1,0:T(8,128)(2,1)S(1)}, u32[]{:S(2)}, u32[]{:S(2)}) collective-permute-start(bf16[1024,128]{1,0:T(8,128)(2,1)S(1)} %pad_maximum_fusion.2), channel_id=1, source_target_pairs={{0,4},{1,5},{2,6},{3,7},{4,0},{5,1},{6,2},{7,3},{8,12},{9,13},{10,... | collective-permute-start | bytes 786440 | tf_op jit(solution)/shard_map/ppermute | solution.py:328
  17.5 0.1 collective-permute-start.7
  18.3 5.5 %receivers.1 = (bf16[256,256]{1,0:T(8,128)(2,1)S(1)}, f32[112,32,128]{2,1,0:T(8,128)S(1)}) custom-call(s32[1,256]{1,0:T(1,128)S(1)} %copy-done.6, f32[1,4,256]{2,1,0:T(4,128)S(1)} %copy-done.4), custom_call_target="tpu_custom_call" | custom-call | tf_op jit(solution)/shard_map/receivers/pallas_call | solution.py:351
  23.9 0.5 collective-permute-done.4.refs_10_
  24.3 0.1 collective-permute-done.5.refs_11_
  24.4 8.0 %forward.1 = (f32[3,48,32,128]{3,2,1,0:T(8,128)S(1)}, f32[48,32,128]{2,1,0:T(8,128)S(1)}, f32[4,20,32,128]{3,2,1,0:T(8,128)S(1)}, bf16[512,128]{1,0:T(8,128)(2,1)}, f32[16,32,128]{2,1,0:T(8,128)S(1)}) custom-call(s32[1,2]{1,0:T(1,128)S(1)} %copy-done.5, s32[1]{0:T(128)S(6)} %copy.14.refs_1_, f32[1,4]{1,0:T(1,128)S(1)} %copy-done.7, ...), custom_call_target="tpu_custom_call" | custom-call | tf_op jit(solution)/shard_map/forward/pallas_call | solution.py:365
  32.4 6.8 %adjoint.1 = (f32[4,128,128]{2,1,0:T(8,128)S(1)}, bf16[512,128]{1,0:T(8,128)(2,1)}) custom-call(s32[1,2]{1,0:T(1,128)S(1)} %copy-done.5, f32[16,32,128]{2,1,0:T(8,128)S(1)} %get-tuple-element.13.refs_1_, bf16[256,256]{1,0:T(8,128)(2,1)S(1)} %get-tuple-element.12.refs_7_.refs_2_, f32[3,48,32,128]{3,2,1,0:T(8,128)S(1)} %get-tuple-element.14.refs_3_, ...), custom_call_target="tpu_custom_call" | custom-call | tf_op jit(solution)/shard_map/adjoint/pallas_call | solution.py:394
  39.2 0.1 collective-permute-start.8
  39.3 1.3 %collective-permute-done.8 = f32[2,128,128]{2,1,0:T(8,128)S(1)} collective-permute-done((f32[2,128,128]{2,1,0:T(8,128)S(1)}, f32[2,128,128]{2,1,0:T(8,128)S(1)}, u32[]{:S(2)}, u32[]{:S(2)}) %collective-permute-start.8) | collective-permute-done | bytes 131104 | tf_op jit(solution)/shard_map/ppermute | solution.py:331
  40.6 0.6 %collective-permute-start.9 = (f32[1,128,128]{2,1,0:T(8,128)S(1)}, f32[1,128,128]{2,1,0:T(8,128)S(1)}, u32[]{:S(2)}, u32[]{:S(2)}) collective-permute-start(f32[1,128,128]{2,1,0:T(8,128)S(1)} %slice.27), channel_id=1, source_target_pairs={{0,2},{1,3},{2,0},{3,1},{4,6},{5,7},{6,4},{7,5},{8,10},{9,11},{10,... | collective-permute-start | bytes 196616 | tf_op jit(solution)/shard_map/ppermute | solution.py:331
  41.2 3.7 %collective-permute-done.9 = f32[1,128,128]{2,1,0:T(8,128)S(1)} collective-permute-done((f32[1,128,128]{2,1,0:T(8,128)S(1)}, f32[1,128,128]{2,1,0:T(8,128)S(1)}, u32[]{:S(2)}, u32[]{:S(2)}) %collective-permute-start.9) | collective-permute-done | bytes 65568 | tf_op jit(solution)/shard_map/ppermute | solution.py:331
  45.0 0.6 %fusion = f32[16,8,128]{2,1,0:T(8,128)} fusion(f32[1,128,128]{2,1,0:T(8,128)S(1)} %collective-permute-done.9, f32[2,128,128]{2,1,0:T(8,128)S(1)} %slice_add_fusion), kind=kLoop, calls=%fused_computation.8 | loop fusion | flops 16384 | bytes 196608 | tf_op jit(solution)/shard_map/reshape;squeeze | solution.py:412
  (25 shorter events, 0.2 us)
Async XLA Ops:
  0.6 23.8 %copy-start.2 = (bf16[1,16,32,128]{3,2,1,0:T(8,128)(2,1)S(1)}, bf16[1,16,32,128]{3,2,1,0:T(8,128)(2,1)}, u32[]{:S(2)}) copy-start(bf16[1,16,32,128]{3,2,1,0:T(8,128)(2,1)} %param.13) | copy-start | bytes 393220
  0.6 23.8 %copy-start.3 = (bf16[1,16,32,128]{3,2,1,0:T(8,128)(2,1)S(1)}, bf16[1,16,32,128]{3,2,1,0:T(8,128)(2,1)}, u32[]{:S(2)}) copy-start(bf16[1,16,32,128]{3,2,1,0:T(8,128)(2,1)} %param.14) | copy-start | bytes 393220
  0.7 14.8 %copy-start = (bf16[1,16,32,128]{3,2,1,0:T(8,128)(2,1)S(1)}, bf16[1,16,32,128]{3,2,1,0:T(8,128)(2,1)}, u32[]{:S(2)}) copy-start(bf16[1,16,32,128]{3,2,1,0:T(8,128)(2,1)} %param.15) | copy-start | bytes 393220
  0.7 14.7 %copy-start.1 = (bf16[1,16,32,128]{3,2,1,0:T(8,128)(2,1)S(1)}, bf16[1,16,32,128]{3,2,1,0:T(8,128)(2,1)}, u32[]{:S(2)}) copy-start(bf16[1,16,32,128]{3,2,1,0:T(8,128)(2,1)} %param.16) | copy-start | bytes 393220
  0.7 17.6 %copy-start.6 = (s32[1,256]{1,0:T(1,128)S(1)}, s32[1,256]{1,0:T(1,128)}, u32[]{:S(2)}) copy-start(s32[1,256]{1,0:T(1,128)} %refs_0_.3) | copy-start | bytes 3076
  0.7 17.6 %copy-start.4 = (f32[1,4,256]{2,1,0:T(4,128)S(1)}, f32[1,4,256]{2,1,0:T(4,128)}, u32[]{:S(2)}) copy-start(f32[1,4,256]{2,1,0:T(4,128)} %refs_1_.2) | copy-start | bytes 12292
  0.7 23.7 %copy-start.7 = (f32[1,4]{1,0:T(1,128)S(1)}, f32[1,4]{1,0:T(1,128)}, u32[]{:S(2)}) copy-start(f32[1,4]{1,0:T(1,128)} %refs_2_.1) | copy-start | bytes 52
  0.7 23.7 %copy-start.5 = (s32[1,2]{1,0:T(1,128)S(1)}, s32[1,2]{1,0:T(1,128)}, u32[]{:S(2)}) copy-start(s32[1,2]{1,0:T(1,128)} %refs_0_.5) | copy-start | bytes 28
  1.6 4.3 %collective-permute-start = (bf16[256,128]{1,0:T(8,128)(2,1)S(1)}, bf16[256,128]{1,0:T(8,128)(2,1)S(1)}, u32[]{:S(2)}, u32[]{:S(2)}) collective-permute-start(bf16[256,128]{1,0:T(8,128)(2,1)S(1)} %pad_maximum_fusion.4), channel_id=1, source_target_pairs={{0,4},{1,5},{2,6},{3,7},{4,0},{5,1},{6,2},{7,3},{8,12},{9,13},{10,... | collective-permute-start | bytes 196616 | tf_op jit(solution)/shard_map/ppermute | solution.py:328
  3.2 4.3 %collective-permute-start.1 = (bf16[256,128]{1,0:T(8,128)(2,1)S(1)}, bf16[256,128]{1,0:T(8,128)(2,1)S(1)}, u32[]{:S(2)}, u32[]{:S(2)}) collective-permute-start(bf16[256,128]{1,0:T(8,128)(2,1)S(1)} %pad_maximum_fusion.4), channel_id=1, source_target_pairs={{0,1},{1,0},{2,3},{3,2},{4,8},{5,9},{6,10},{7,11},{8,4},{9,5},{10,... | collective-permute-start | bytes 196616 | tf_op jit(solution)/shard_map/ppermute | solution.py:328
  8.3 5.7 %collective-permute-start.2 = (bf16[768,128]{1,0:T(8,128)(2,1)S(1)}, bf16[768,128]{1,0:T(8,128)(2,1)S(1)}, u32[]{:S(2)}, u32[]{:S(2)}) collective-permute-start(bf16[768,128]{1,0:T(8,128)(2,1)S(1)} %get-tuple-element.24.refs_3_), channel_id=1, source_target_pairs={{0,2},{1,3},{2,0},{3,1},{4,6},{5,7},{6,4},{7,5},{8,10},{9,11},{10,... | collective-permute-start | bytes 589832 | tf_op jit(solution)/shard_map/ppermute | solution.py:331
  14.1 9.7 %collective-permute-start.3 = (bf16[2,768,128]{2,1,0:T(8,128)(2,1)S(1)}, bf16[2,768,128]{2,1,0:T(8,128)(2,1)S(1)}, u32[]{:S(2)}, u32[]{:S(2)}) collective-permute-start(bf16[2,768,128]{2,1,0:T(8,128)(2,1)S(1)} %pad_maximum_fusion), channel_id=1, source_target_pairs={{0,1},{1,0},{2,3},{3,2},{4,5},{5,4},{6,7},{7,6},{8,9},{9,8},{10,11... | collective-permute-start | bytes 1179656 | tf_op jit(solution)/shard_map/ppermute | solution.py:331
  15.1 9.2 %collective-permute-start.4 = (bf16[1024,128]{1,0:T(8,128)(2,1)S(1)}, bf16[1024,128]{1,0:T(8,128)(2,1)S(1)}, u32[]{:S(2)}, u32[]{:S(2)}) collective-permute-start(bf16[1024,128]{1,0:T(8,128)(2,1)S(1)} %pad_maximum_fusion.1), channel_id=1, source_target_pairs={{0,4},{1,5},{2,6},{3,7},{4,0},{5,1},{6,2},{7,3},{8,12},{9,13},{10,... | collective-permute-start | bytes 786440 | tf_op jit(solution)/shard_map/ppermute | solution.py:328
  15.2 9.2 %collective-permute-start.5 = (bf16[1024,128]{1,0:T(8,128)(2,1)S(1)}, bf16[1024,128]{1,0:T(8,128)(2,1)S(1)}, u32[]{:S(2)}, u32[]{:S(2)}) collective-permute-start(bf16[1024,128]{1,0:T(8,128)(2,1)S(1)} %pad_maximum_fusion.1), channel_id=1, source_target_pairs={{0,1},{1,0},{2,3},{3,2},{4,8},{5,9},{6,10},{7,11},{8,4},{9,5},{10,... | collective-permute-start | bytes 786440 | tf_op jit(solution)/shard_map/ppermute | solution.py:328
  15.4 16.9 %collective-permute-start.6 = (bf16[1024,128]{1,0:T(8,128)(2,1)S(1)}, bf16[1024,128]{1,0:T(8,128)(2,1)S(1)}, u32[]{:S(2)}, u32[]{:S(2)}) collective-permute-start(bf16[1024,128]{1,0:T(8,128)(2,1)S(1)} %pad_maximum_fusion.2), channel_id=1, source_target_pairs={{0,4},{1,5},{2,6},{3,7},{4,0},{5,1},{6,2},{7,3},{8,12},{9,13},{10,... | collective-permute-start | bytes 786440 | tf_op jit(solution)/shard_map/ppermute | solution.py:328
  17.5 14.8 %collective-permute-start.7 = (bf16[1024,128]{1,0:T(8,128)(2,1)S(1)}, bf16[1024,128]{1,0:T(8,128)(2,1)S(1)}, u32[]{:S(2)}, u32[]{:S(2)}) collective-permute-start(bf16[1024,128]{1,0:T(8,128)(2,1)S(1)} %pad_maximum_fusion.2), channel_id=1, source_target_pairs={{0,1},{1,0},{2,3},{3,2},{4,8},{5,9},{6,10},{7,11},{8,4},{9,5},{10,... | collective-permute-start | bytes 786440 | tf_op jit(solution)/shard_map/ppermute | solution.py:328
  39.2 1.4 %collective-permute-start.8 = (f32[2,128,128]{2,1,0:T(8,128)S(1)}, f32[2,128,128]{2,1,0:T(8,128)S(1)}, u32[]{:S(2)}, u32[]{:S(2)}) collective-permute-start(f32[2,128,128]{2,1,0:T(8,128)S(1)} %slice.21), channel_id=1, source_target_pairs={{0,1},{1,0},{2,3},{3,2},{4,5},{5,4},{6,7},{7,6},{8,9},{9,8},{10,11... | collective-permute-start | bytes 393224 | tf_op jit(solution)/shard_map/ppermute | solution.py:331
  40.6 4.3 %collective-permute-start.9 = (f32[1,128,128]{2,1,0:T(8,128)S(1)}, f32[1,128,128]{2,1,0:T(8,128)S(1)}, u32[]{:S(2)}, u32[]{:S(2)}) collective-permute-start(f32[1,128,128]{2,1,0:T(8,128)S(1)} %slice.27), channel_id=1, source_target_pairs={{0,2},{1,3},{2,0},{3,1},{4,6},{5,7},{6,4},{7,5},{8,10},{9,11},{10,... | collective-permute-start | bytes 196616 | tf_op jit(solution)/shard_map/ppermute | solution.py:331

commit v2 on v1

--- a/solution.py
+++ b/solution.py
@@ -61,8 +61,12 @@
     return low, high
 
 
-def setup_kernel(cx, cells_ref, traces_ref, weights_ref, add_ref):
-    ny, nz = 32, 128
+def setup_kernel(cx, cells_ref, traces_ref, *refs):
+    parts, (weights_ref, add_ref, joined_ref) = refs[:-3], refs[-3:]
+    ny, nz = add_ref.shape[2:]
+    size = parts[0].shape[0]
+    for number, part in enumerate(parts):
+        joined_ref[number * size : (number + 1) * size, :] = part[...]
     rows = lax.broadcasted_iota(jnp.int32, (2 * nz, 2 * nz), 0)
     cols = lax.broadcasted_iota(jnp.int32, (2 * nz, 2 * nz), 1)
     ahead = lax.rem(rows, nz) - lax.rem(cols, nz)
@@ -76,30 +80,29 @@
     tile = lax.axis_index("tile")
     count = cells_ref.shape[1]
     cells = cells_ref[...]
-    at_row = cells // nz - (tile - 1) * (cx * ny)
+    reach = (STEPS - 1) * HALO
+    at_row = cells // nz - (tile * cx - reach) * ny
     at_z = lax.rem(cells, nz)
     depth = lax.broadcasted_iota(jnp.int32, (nz, count), 0)
-    depth_hot = jnp.where(depth == at_z, 1.0, 0.0).astype(jnp.bfloat16)
-    depth_hot = jnp.concatenate([depth_hot, depth_hot], axis=1)
-    block = HALO * ny
-    row = lax.broadcasted_iota(jnp.int32, (block, count), 0)
-    base = 0
+    deep = depth == at_z
+    values = []
     for step in range(STEPS):
-        reach = (STEPS - 1 - step) * HALO
-        layers = cx + 2 * reach
         trace = traces_ref[0, pl.ds(STEPS - 1 - step, 1), :]
         high = trace.astype(jnp.bfloat16).astype(jnp.float32)
-        low = trace - high
-
-        def body(c, carry, base=base, reach=reach, high=high, low=low):
-            hot = at_row == row + (cx - reach + c * HALO) * ny
-            spread = jnp.concatenate([jnp.where(hot, high, 0.0), jnp.where(hot, low, 0.0)], axis=1).astype(jnp.bfloat16)
-            value = lax.dot_general(spread, depth_hot, (((1,), (1,)), ((), ())), preferred_element_type=jnp.float32)
-            add_ref[pl.ds(base + c * HALO, HALO)] = value.reshape(HALO, ny, nz)
-            return carry
-
-        lax.fori_loop(0, layers // HALO, body, 0)
-        base += layers
+        values += [jnp.where(deep, high, 0.0), jnp.where(deep, trace - high, 0.0)]
+    values = jnp.concatenate(values, axis=0).astype(jnp.bfloat16)
+    chunk = 2 * HALO
+    row = lax.broadcasted_iota(jnp.int32, (chunk * ny, count), 0)
+
+    def body(c, carry):
+        hot = jnp.where(at_row == row + c * (chunk * ny), 1.0, 0.0).astype(jnp.bfloat16)
+        found = lax.dot_general(hot, values, (((1,), (1,)), ((), ())), preferred_element_type=jnp.float32)
+        for step in range(STEPS):
+            both = found[:, 2 * step * nz : (2 * step + 1) * nz] + found[:, (2 * step + 1) * nz : (2 * step + 2) * nz]
+            add_ref[step, pl.ds(c * chunk, chunk)] = both.reshape(chunk, ny, nz)
+        return carry
+
+    lax.fori_loop(0, (cx + 2 * reach) // chunk, body, 0)
 
 
 def differences(buf, i0, weights, ny):
@@ -176,16 +179,14 @@
         buf[2 * cx : 2 * cx + HALO, PAD : PAD + ny, :] = zero
 
 
-def forward_kernel(
-    cx, ny, nz, order, aperture_ref, source_ref, wavelet_ref, *refs
-):
-    model_refs = refs[: len(order)]
-    weights_ref, own_now, own_before, from_a, from_b = refs[len(order) : len(order) + 5]
-    slopes_ref, courant_ref, stored_ref, end_ref, gain_ref, log_buf, now, before = refs[len(order) + 5 :]
+def forward_kernel(cx, ny, nz, shots, blocks, aperture_ref, source_ref, wavelet_ref, *refs):
+    model_refs = refs[: len(blocks)]
+    weights_ref, own_now, own_before, from_a, from_b = refs[len(blocks) : len(blocks) + 5]
+    slopes_ref, courant_ref, stored_ref, end_ref, gain_ref, log_buf, now, before = refs[len(blocks) + 5 :]
     tile, own, left, right, side_a, side_b = layout(aperture_ref, cx)
     shot = lax.axis_index("shot")
     sides = ((cx, None), (side_a[0], side_a[1]), (side_b[0], side_b[1]))
-    block_rows = ny // len(order)
+    block_rows = ny // shots
     size = cx * block_rows
 
     @pl.when(jnp.logical_not(own))
@@ -197,10 +198,11 @@
         zero = jnp.zeros((3 * cx, PAD, nz), jnp.float32)
         log_buf[:, 0:PAD, :] = zero
         log_buf[:, PAD + ny : 2 * PAD + ny, :] = zero
-        for ref, mask in zip(model_refs, order):
-            y0 = pl.multiple_of((shot ^ mask) * block_rows, block_rows)
-            for place, (at, here) in enumerate(sides):
-                base = place * 2 * size
+        for ref, held in zip(model_refs, blocks):
+            for number, (mask, place) in enumerate(held):
+                y0 = pl.multiple_of((shot ^ mask) * block_rows, block_rows)
+                at, here = sides[place]
+                base = number * 2 * size
                 speed = ref[pl.ds(base, size), :].astype(jnp.float32)
                 courant = (speed * speed) * (1.0 / SCALE)
                 courant_ref[pl.ds(at, cx), pl.ds(y0, block_rows), :] = courant.reshape(cx, block_rows, nz)
@@ -273,14 +275,12 @@
         fill_fields(now, before, own_now, own_before, from_a, from_b, side_a, side_b, cx, ny, nz)
         weights = weights_ref[...]
         bufs = (now, before)
-        base = 0
         for step in range(STEPS):
             cur, prev = bufs[step % 2], bufs[(step + 1) % 2]
             span = bounds(step, left, right, cx)
-            reach = (STEPS - 1 - step) * HALO
-
-            def use(c, j, applied, updated, step=step, base=base, reach=reach):
-                updated = updated + add_ref[base + reach - cx + c * HALO + j]
+
+            def use(c, j, applied, updated, step=step):
+                updated = updated + add_ref[step, c * HALO + j - (cx - (STEPS - 1) * HALO)]
                 inner = (c >= cx // HALO) & (c < 2 * cx // HALO)
                 at = jnp.where(inner, c * HALO - cx, cx)
                 term = updated * stored_ref[STEPS - 1 - step, at + j]
@@ -290,7 +290,6 @@
             march(step, cur, prev, slopes_ref, courant_ref, weights, span, cx, ny, use)
             if step == 0:
                 clear_sides(cur, left, right, cx, ny, nz)
-            base += cx + 2 * reach
         last = bufs[STEPS % 2]
         start_ref[...] = last[cx : 2 * cx, PAD : PAD + ny, :].reshape(cx * ny, nz).astype(jnp.bfloat16)
         for place, mask in enumerate(order):
@@ -333,37 +332,49 @@
     model = jnp.concatenate([velocity.reshape(-1, nz), density.reshape(-1, nz)], axis=0)
     model_a, model_b = swap(model, "a"), swap(model, "b")
     forward = jnp.concatenate([wave_now.reshape(rows, nz), wave_before.reshape(rows, nz)], axis=0)
-    forward_a, forward_b = swap(forward, "a"), swap(forward, "b")
+    high = shots // 2
+    near = [([(0, 0)], model), ([(0, 1)], model_a), ([(0, 2)], model_b)]
+    late = []
+    if high:
+        model_c = cross(model, high)
+        forward_a, forward_b = swap(forward, "a"), swap(forward, "b")
+        near.append(([(high, 0)], model_c))
+        late.append(([(high, 1), (high, 2)], cross(jnp.concatenate([model_a, model_b], axis=0), high)))
+    else:
+        forward_a, forward_b = swap(forward, "a"), swap(forward, "b")
+    mask = high // 2
     adjoint = jnp.concatenate([adjoint_end.reshape(rows, nz), adjoint_after.reshape(rows, nz)], axis=0)
     adjoint_a, adjoint_b = swap(adjoint, "a"), swap(adjoint, "b")
 
-    held = [(0, jnp.concatenate([model, model_a, model_b], axis=0))]
-    mask = shots // 2
-    while mask:
-        if len(held) > 1:
-            moved = cross(jnp.stack([block for _, block in held]), mask)
-            held = held + [(m ^ mask, moved[i]) for i, (m, _) in enumerate(held)]
-        else:
-            held = held + [(mask, cross(held[0][1], mask))]
-        mask //= 2
-
-    added_layers = sum(cx + 2 * (STEPS - 1 - step) * HALO for step in range(STEPS))
-    weights, added = pl.pallas_call(
+    weights, added, joined = pl.pallas_call(
         lambda *refs: setup_kernel(cx, *refs),
         out_shape=(
             jax.ShapeDtypeStruct((2 * nz, 2 * nz), jnp.bfloat16),
-            jax.ShapeDtypeStruct((added_layers, ny, nz), jnp.float32),
+            jax.ShapeDtypeStruct((STEPS, cx + 2 * (STEPS - 1) * HALO, ny, nz), jnp.float32),
+            jax.ShapeDtypeStruct((len(near) * model.shape[0], nz), jnp.bfloat16),
         ),
-        in_specs=[vmem()] * 2,
-        out_specs=(vmem(), vmem()),
+        in_specs=[vmem()] * (2 + len(near)),
+        out_specs=(vmem(),) * 3,
         compiler_params=params,
+        cost_estimate=pl.CostEstimate(flops=2 * 10**9, bytes_accessed=4 * 2**20, transcendentals=0),
         name="receivers",
-    )(receiver_cell, residual_traces)
-
-    order = tuple(m for m, _ in held)
+    )(receiver_cell, residual_traces, *[block for _, block in near])
+
+    near = [([name for names, _ in near for name in names], joined)]
+    while mask:
+        moved = []
+        for group in (near, late):
+            names = [(m ^ mask, place) for held, _ in group for m, place in held]
+            array = group[0][1] if len(group) == 1 else jnp.concatenate([block for _, block in group], axis=0)
+            moved.append((names, cross(array, mask)))
+        near, late = near + moved[:1], late + moved[1:]
+        mask //= 2
+    held = near + late
+
     field = pltpu.VMEM((3 * cx, 2 * PAD + ny, nz), jnp.float32)
+    blocks = tuple(tuple(names) for names, _ in held)
     slopes, courant, stored, wave_end, gain = pl.pallas_call(
-        lambda *refs: forward_kernel(cx, ny, nz, order, *refs),
+        lambda *refs: forward_kernel(cx, ny, nz, shots, blocks, *refs),
         out_shape=(
             jax.ShapeDtypeStruct((3, 3 * cx, ny, nz), jnp.float32),
             jax.ShapeDtypeStruct((3 * cx, ny, nz), jnp.float32),
@@ -371,10 +382,11 @@
             jax.ShapeDtypeStruct((rows, nz), jnp.bfloat16),
             jax.ShapeDtypeStruct((cx, ny, nz), jnp.float32),
         ),
-        in_specs=[smem()] * 3 + [vmem()] * (len(order) + 5),
+        in_specs=[smem()] * 3 + [vmem()] * (len(held) + 5),
         out_specs=(vmem(),) * 5,
         scratch_shapes=[field, field, field],
         compiler_params=params,
+        cost_estimate=pl.CostEstimate(flops=5 * 10**9, bytes_accessed=8 * 2**20, transcendentals=0),
         name="forward",
     )(
         aperture, source_cell, source_wave, *[block for _, block in held], weights,
@@ -401,6 +413,7 @@
         out_specs=(vmem(),) * 2,
         scratch_shapes=[field, field, pltpu.VMEM((cx + HALO, ny, nz), jnp.float32)],
         compiler_params=params,
+        cost_estimate=pl.CostEstimate(flops=5 * 10**9, bytes_accessed=8 * 2**20, transcendentals=0),
         name="adjoint",
     )(
         aperture, gain, weights, slopes, courant, stored, added, adjoint_end.reshape(rows, nz), adjoint_after.reshape(rows, nz),

time: 46.3 us -> 37.9 us (0.82); the launches traced: 45.6 us -> 37.8 us
  waiting for transfers between devices: 14 us -> 5.67 us
  starting transfers between devices: 6.38 us -> 10.1 us
  Pallas kernels: 20.2 us -> 16.7 us
  local copies, waits for them, and re-layouts: 0.08 us -> 1.42 us
  other arithmetic: 3.43 us -> 2.45 us
    ppermute x6, waiting for transfers between devices: 4.8 us -> 0.02 us  [swap(): return lax.ppermute(x, ('tile', 'shot'), pairs((tiles, shots), kind))]
    pallas_call x1, Pallas kernels: 5.47 us -> 1.85 us  [local(): pl.pallas_call(lambda *refs: setup_kernel(cx, *refs), out_shape=(jax.Shap...]
    ppermute x4 -> x6, waiting for transfers between devices: 9.23 us -> 5.66 us  [cross(): return lax.ppermute(x, 'shot', [(i, i ^ mask) for i in range(shots)])]
    ppermute x6, starting transfers between devices: 4.06 us -> 6.77 us  [swap(): return lax.ppermute(x, ('tile', 'shot'), pairs((tiles, shots), kind))]
    unnamed x16, local copies, waits for them, and re-layouts: 0.04 us -> 1.4 us
    ppermute x4 -> x6, starting transfers between devices: 2.31 us -> 3.38 us  [cross(): return lax.ppermute(x, 'shot', [(i, i ^ mask) for i in range(shots)])]
    another operation x2 -> x0, other arithmetic: 0.85 us -> none  [local(): moved = cross(jnp.stack([block for _, block in held]), mask)]
  transfers between devices with their start and end apart: 10 -> 12, of which waited for: 7 -> 3; matrix products, arithmetic and copies ran while one was open for 2% -> 3% of each run, Pallas kernels for 29% -> 26%
where the time goes in v2:
time: 37.9 us; the launch traced here: 37.8 us
  Pallas kernels  16.7 us (44%)
  starting transfers between devices  10.1 us (27%)
  waiting for transfers between devices  5.67 us (15%)
  other arithmetic  2.45 us (6%)
  between operations  1.44 us (4%)
  local copies, waits for them, and re-layouts  1.42 us (4%)
    pallas_call x1, Pallas kernels, local(): pl.pallas_call(lambda *refs: forward_kernel(cx, ny, nz, shots, blocks, *r...  7.98 us
    pallas_call x1, Pallas kernels, local(): pl.pallas_call(lambda *refs: adjoint_kernel(cx, ny, nz, sum_order, *refs)...  6.84 us
    ppermute x6, starting transfers between devices, swap(): return lax.ppermute(x, ('tile', 'shot'), pairs((tiles, shots), kind))  6.77 us
    ppermute x6, waiting for transfers between devices, cross(): return lax.ppermute(x, 'shot', [(i, i ^ mask) for i in range(shots)])  5.66 us
    ppermute x6, starting transfers between devices, cross(): return lax.ppermute(x, 'shot', [(i, i ^ mask) for i in range(shots)])  3.38 us
    pallas_call x1, Pallas kernels, local(): pl.pallas_call(lambda *refs: setup_kernel(cx, *refs), out_shape=(jax.Shap...  1.85 us
    unnamed x16, local copies, waits for them, and re-layouts  1.4 us
    concatenate x1, other arithmetic, local(): jnp.concatenate([wave_now.reshape(rows, nz), wave_before.reshape(rows, nz...  0.99 us
  transfers between devices with their start and end apart: 12, of which 3 were waited for; matrix products, arithmetic and copies ran while one was open for 3% of the time, Pallas kernels for 26%

profile of v2, /device:TPU:16, one launch (start us, length us, event | category | flops | bytes accessed | tf_op | source)
XLA Modules:
  0.0 37.8 jit_solution(9946798790428186270)
XLA Ops:
  0.6 0.8 %pad_maximum_fusion.3.refs_2_ = bf16[256,128]{1,0:T(8,128)(2,1)S(1)} fusion(bf16[128,128]{1,0:T(8,128)(2,1)} %bitcast.18, bf16[128,128]{1,0:T(8,128)(2,1)} %bitcast.19), kind=kLoop, calls=%fused_computation.6 | loop fusion | flops 131072 | bytes 131072 | tf_op jit(solution)/shard_map/concatenate | solution.py:332
  1.4 1.6 %collective-permute-start = (bf16[256,128]{1,0:T(8,128)(2,1)S(1)}, bf16[256,128]{1,0:T(8,128)(2,1)S(1)}, u32[]{:S(2)}, u32[]{:S(2)}) collective-permute-start(bf16[256,128]{1,0:T(8,128)(2,1)S(1)} %pad_maximum_fusion.3.refs_2_), channel_id=1, source_target_pairs={{0,4},{1,5},{2,6},{3,7},{4,0},{5,1},{6,2},{7,3},{8,12},{9,13},{10,... | collective-permute-start | bytes 196616 | tf_op jit(solution)/shard_map/ppermute | solution.py:327
  3.0 1.5 %collective-permute-start.2 = (bf16[256,128]{1,0:T(8,128)(2,1)S(1)}, bf16[256,128]{1,0:T(8,128)(2,1)S(1)}, u32[]{:S(2)}, u32[]{:S(2)}) collective-permute-start(bf16[256,128]{1,0:T(8,128)(2,1)S(1)} %pad_maximum_fusion.3.refs_2_), channel_id=1, source_target_pairs={{0,2},{1,3},{2,0},{3,1},{4,6},{5,7},{6,4},{7,5},{8,10},{9,11},{10,... | collective-permute-start | bytes 196616 | tf_op jit(solution)/shard_map/ppermute | solution.py:330
  4.5 1.0 %pad_maximum_fusion = bf16[1024,128]{1,0:T(8,128)(2,1)S(1)} fusion(bf16[512,128]{1,0:T(8,128)(2,1)} %bitcast.12, bf16[512,128]{1,0:T(8,128)(2,1)} %bitcast.10), kind=kLoop, calls=%fused_computation | loop fusion | flops 524288 | bytes 524288 | tf_op jit(solution)/shard_map/concatenate | solution.py:334
  5.5 0.5 %collective-permute-start.6 = (bf16[1024,128]{1,0:T(8,128)(2,1)S(1)}, bf16[1024,128]{1,0:T(8,128)(2,1)S(1)}, u32[]{:S(2)}, u32[]{:S(2)}) collective-permute-start(bf16[1024,128]{1,0:T(8,128)(2,1)S(1)} %pad_maximum_fusion), channel_id=1, source_target_pairs={{0,4},{1,5},{2,6},{3,7},{4,0},{5,1},{6,2},{7,3},{8,12},{9,13},{10,... | collective-permute-start | bytes 786440 | tf_op jit(solution)/shard_map/ppermute | solution.py:327
  6.0 1.7 %collective-permute-start.7 = (bf16[1024,128]{1,0:T(8,128)(2,1)S(1)}, bf16[1024,128]{1,0:T(8,128)(2,1)S(1)}, u32[]{:S(2)}, u32[]{:S(2)}) collective-permute-start(bf16[1024,128]{1,0:T(8,128)(2,1)S(1)} %pad_maximum_fusion), channel_id=1, source_target_pairs={{0,1},{1,0},{2,3},{3,2},{4,8},{5,9},{6,10},{7,11},{8,4},{9,5},{10,... | collective-permute-start | bytes 786440 | tf_op jit(solution)/shard_map/ppermute | solution.py:327
  7.7 0.0 copy-start.7
  7.7 0.0 copy-start.2
  7.7 0.0 copy-start.3
  7.7 1.1 %collective-permute-start.4 = (bf16[512,128]{1,0:T(8,128)(2,1)S(1)}, bf16[512,128]{1,0:T(8,128)(2,1)S(1)}, u32[]{:S(2)}, u32[]{:S(2)}) collective-permute-start(bf16[512,128]{1,0:T(8,128)(2,1)S(1)} %pad_maximum_fusion.2), channel_id=1, source_target_pairs={{0,2},{1,3},{2,0},{3,1},{4,6},{5,7},{6,4},{7,5},{8,10},{9,11},{10,... | collective-permute-start | bytes 393224 | tf_op jit(solution)/shard_map/ppermute | solution.py:330
  8.9 0.7 %copy-done.4 = f32[1,4,256]{2,1,0:T(4,128)S(1)} copy-done((f32[1,4,256]{2,1,0:T(4,128)S(1)}, f32[1,4,256]{2,1,0:T(4,128)}, u32[]{:S(2)}) %copy-start.4) | copy-done | bytes 4120
  9.6 0.7 %copy-done.5 = s32[1,256]{1,0:T(1,128)S(1)} copy-done((s32[1,256]{1,0:T(1,128)S(1)}, s32[1,256]{1,0:T(1,128)}, u32[]{:S(2)}) %copy-start.5) | copy-done | bytes 1048
  10.2 1.9 %receivers.1 = (bf16[256,256]{1,0:T(8,128)(2,1)S(1)}, f32[4,40,32,128]{3,2,1,0:T(8,128)S(1)}, bf16[1024,128]{1,0:T(8,128)(2,1)S(1)}) custom-call(s32[1,256]{1,0:T(1,128)S(1)} %copy-done.5, f32[1,4,256]{2,1,0:T(4,128)S(1)} %copy-done.4, bf16[256,128]{1,0:T(8,128)(2,1)S(1)} %pad_maximum_fusion.3.refs_2_, bf16[256,128]{1,0:T(8,128)(2,1)S(1)} %collective-permute-done.refs_3_, ...), custom_call_target="tpu_custom_call" | custom-call | flops 2000000000 | bytes 4194304 | tf_op jit(solution)/shard_map/receivers/pallas_call | solution.py:349
  12.1 0.1 collective-permute-start.3
  12.2 0.6 %collective-permute-done.4.refs_5_ = bf16[512,128]{1,0:T(8,128)(2,1)S(1)} collective-permute-done((bf16[512,128]{1,0:T(8,128)(2,1)S(1)}, bf16[512,128]{1,0:T(8,128)(2,1)S(1)}, u32[]{:S(2)}, u32[]{:S(2)}) %collective-permute-start.4) | collective-permute-done | bytes 131104 | tf_op jit(solution)/shard_map/ppermute | solution.py:330
  12.8 0.9 %collective-permute-start.8 = (bf16[1024,128]{1,0:T(8,128)(2,1)S(1)}, bf16[1024,128]{1,0:T(8,128)(2,1)S(1)}, u32[]{:S(2)}, u32[]{:S(2)}) collective-permute-start(bf16[1024,128]{1,0:T(8,128)(2,1)S(1)} %pad_maximum_fusion.1), channel_id=1, source_target_pairs={{0,4},{1,5},{2,6},{3,7},{4,0},{5,1},{6,2},{7,3},{8,12},{9,13},{10,... | collective-permute-start | bytes 786440 | tf_op jit(solution)/shard_map/ppermute | solution.py:327
  14.4 2.1 %collective-permute-start.9 = (bf16[1024,128]{1,0:T(8,128)(2,1)S(1)}, bf16[1024,128]{1,0:T(8,128)(2,1)S(1)}, u32[]{:S(2)}, u32[]{:S(2)}) collective-permute-start(bf16[1024,128]{1,0:T(8,128)(2,1)S(1)} %pad_maximum_fusion.1), channel_id=1, source_target_pairs={{0,1},{1,0},{2,3},{3,2},{4,8},{5,9},{6,10},{7,11},{8,4},{9,5},{10,... | collective-permute-start | bytes 786440 | tf_op jit(solution)/shard_map/ppermute | solution.py:327
  16.5 8.0 %forward.1 = (f32[3,48,32,128]{3,2,1,0:T(8,128)S(1)}, f32[48,32,128]{2,1,0:T(8,128)S(1)}, f32[4,20,32,128]{3,2,1,0:T(8,128)S(1)}, bf16[512,128]{1,0:T(8,128)(2,1)}, f32[16,32,128]{2,1,0:T(8,128)S(1)}) custom-call(s32[1,2]{1,0:T(1,128)S(1)} %copy-done.7, s32[1]{0:T(128)S(6)} %copy.14.refs_1_, f32[1,4]{1,0:T(1,128)S(1)} %copy-done.6, ...), custom_call_target="tpu_custom_call" | custom-call | flops 5000000000 | bytes 8388608 | tf_op jit(solution)/shard_map/forward/pallas_call | solution.py:376
  24.5 6.8 %adjoint.1 = (f32[4,128,128]{2,1,0:T(8,128)S(1)}, bf16[512,128]{1,0:T(8,128)(2,1)}) custom-call(s32[1,2]{1,0:T(1,128)S(1)} %copy-done.7, f32[16,32,128]{2,1,0:T(8,128)S(1)} %get-tuple-element.15.refs_1_, bf16[256,256]{1,0:T(8,128)(2,1)S(1)} %get-tuple-element.14.refs_7_.refs_2_, f32[3,48,32,128]{3,2,1,0:T(8,128)S(1)} %get-tuple-element.16.refs_3_, ...), custom_call_target="tpu_custom_call" | custom-call | flops 5000000000 | bytes 8388608 | tf_op jit(solution)/shard_map/adjoint/pallas_call | solution.py:406
  31.4 0.1 collective-permute-start.10
  31.5 1.3 %collective-permute-done.10 = f32[2,128,128]{2,1,0:T(8,128)S(1)} collective-permute-done((f32[2,128,128]{2,1,0:T(8,128)S(1)}, f32[2,128,128]{2,1,0:T(8,128)S(1)}, u32[]{:S(2)}, u32[]{:S(2)}) %collective-permute-start.10) | collective-permute-done | bytes 131104 | tf_op jit(solution)/shard_map/ppermute | solution.py:330
  32.8 0.6 %collective-permute-start.11 = (f32[1,128,128]{2,1,0:T(8,128)S(1)}, f32[1,128,128]{2,1,0:T(8,128)S(1)}, u32[]{:S(2)}, u32[]{:S(2)}) collective-permute-start(f32[1,128,128]{2,1,0:T(8,128)S(1)} %slice.17), channel_id=1, source_target_pairs={{0,2},{1,3},{2,0},{3,1},{4,6},{5,7},{6,4},{7,5},{8,10},{9,11},{10,... | collective-permute-start | bytes 196616 | tf_op jit(solution)/shard_map/ppermute | solution.py:330
  33.4 3.7 %collective-permute-done.11 = f32[1,128,128]{2,1,0:T(8,128)S(1)} collective-permute-done((f32[1,128,128]{2,1,0:T(8,128)S(1)}, f32[1,128,128]{2,1,0:T(8,128)S(1)}, u32[]{:S(2)}, u32[]{:S(2)}) %collective-permute-start.11) | collective-permute-done | bytes 65568 | tf_op jit(solution)/shard_map/ppermute | solution.py:330
  37.2 0.6 %fusion = f32[16,8,128]{2,1,0:T(8,128)} fusion(f32[1,128,128]{2,1,0:T(8,128)S(1)} %collective-permute-done.11, f32[2,128,128]{2,1,0:T(8,128)S(1)} %slice_add_fusion), kind=kLoop, calls=%fused_computation.5 | loop fusion | flops 16384 | bytes 196608 | tf_op jit(solution)/shard_map/reshape;squeeze | solution.py:425
  (27 shorter events, 0.1 us)
Async XLA Ops:
  1.4 6.2 %collective-permute-start = (bf16[256,128]{1,0:T(8,128)(2,1)S(1)}, bf16[256,128]{1,0:T(8,128)(2,1)S(1)}, u32[]{:S(2)}, u32[]{:S(2)}) collective-permute-start(bf16[256,128]{1,0:T(8,128)(2,1)S(1)} %pad_maximum_fusion.3.refs_2_), channel_id=1, source_target_pairs={{0,4},{1,5},{2,6},{3,7},{4,0},{5,1},{6,2},{7,3},{8,12},{9,13},{10,... | collective-permute-start | bytes 196616 | tf_op jit(solution)/shard_map/ppermute | solution.py:327
  3.0 4.7 %collective-permute-start.1 = (bf16[256,128]{1,0:T(8,128)(2,1)S(1)}, bf16[256,128]{1,0:T(8,128)(2,1)S(1)}, u32[]{:S(2)}, u32[]{:S(2)}) collective-permute-start(bf16[256,128]{1,0:T(8,128)(2,1)S(1)} %pad_maximum_fusion.3.refs_2_), channel_id=1, source_target_pairs={{0,1},{1,0},{2,3},{3,2},{4,8},{5,9},{6,10},{7,11},{8,4},{9,5},{10,... | collective-permute-start | bytes 196616 | tf_op jit(solution)/shard_map/ppermute | solution.py:327
  3.0 5.9 %collective-permute-start.2 = (bf16[256,128]{1,0:T(8,128)(2,1)S(1)}, bf16[256,128]{1,0:T(8,128)(2,1)S(1)}, u32[]{:S(2)}, u32[]{:S(2)}) collective-permute-start(bf16[256,128]{1,0:T(8,128)(2,1)S(1)} %pad_maximum_fusion.3.refs_2_), channel_id=1, source_target_pairs={{0,2},{1,3},{2,0},{3,1},{4,6},{5,7},{6,4},{7,5},{8,10},{9,11},{10,... | collective-permute-start | bytes 196616 | tf_op jit(solution)/shard_map/ppermute | solution.py:330
  5.5 8.9 %collective-permute-start.6 = (bf16[1024,128]{1,0:T(8,128)(2,1)S(1)}, bf16[1024,128]{1,0:T(8,128)(2,1)S(1)}, u32[]{:S(2)}, u32[]{:S(2)}) collective-permute-start(bf16[1024,128]{1,0:T(8,128)(2,1)S(1)} %pad_maximum_fusion), channel_id=1, source_target_pairs={{0,4},{1,5},{2,6},{3,7},{4,0},{5,1},{6,2},{7,3},{8,12},{9,13},{10,... | collective-permute-start | bytes 786440 | tf_op jit(solution)/shard_map/ppermute | solution.py:327
  6.0 10.5 %collective-permute-start.7 = (bf16[1024,128]{1,0:T(8,128)(2,1)S(1)}, bf16[1024,128]{1,0:T(8,128)(2,1)S(1)}, u32[]{:S(2)}, u32[]{:S(2)}) collective-permute-start(bf16[1024,128]{1,0:T(8,128)(2,1)S(1)} %pad_maximum_fusion), channel_id=1, source_target_pairs={{0,1},{1,0},{2,3},{3,2},{4,8},{5,9},{6,10},{7,11},{8,4},{9,5},{10,... | collective-permute-start | bytes 786440 | tf_op jit(solution)/shard_map/ppermute | solution.py:327
  7.6 8.9 %copy-start.6 = (f32[1,4]{1,0:T(1,128)S(1)}, f32[1,4]{1,0:T(1,128)}, u32[]{:S(2)}) copy-start(f32[1,4]{1,0:T(1,128)} %refs_2_.1) | copy-start | bytes 52
  7.7 8.9 %copy-start.7 = (s32[1,2]{1,0:T(1,128)S(1)}, s32[1,2]{1,0:T(1,128)}, u32[]{:S(2)}) copy-start(s32[1,2]{1,0:T(1,128)} %refs_0_.5) | copy-start | bytes 28
  7.7 5.1 %copy-start.2 = (bf16[1,16,32,128]{3,2,1,0:T(8,128)(2,1)S(1)}, bf16[1,16,32,128]{3,2,1,0:T(8,128)(2,1)}, u32[]{:S(2)}) copy-start(bf16[1,16,32,128]{3,2,1,0:T(8,128)(2,1)} %param.15) | copy-start | bytes 393220
  7.7 5.1 %copy-start.3 = (bf16[1,16,32,128]{3,2,1,0:T(8,128)(2,1)S(1)}, bf16[1,16,32,128]{3,2,1,0:T(8,128)(2,1)}, u32[]{:S(2)}) copy-start(bf16[1,16,32,128]{3,2,1,0:T(8,128)(2,1)} %param.16) | copy-start | bytes 393220
  7.7 8.8 %copy-start = (bf16[1,16,32,128]{3,2,1,0:T(8,128)(2,1)S(1)}, bf16[1,16,32,128]{3,2,1,0:T(8,128)(2,1)}, u32[]{:S(2)}) copy-start(bf16[1,16,32,128]{3,2,1,0:T(8,128)(2,1)} %param.13) | copy-start | bytes 393220
  7.7 8.8 %copy-start.1 = (bf16[1,16,32,128]{3,2,1,0:T(8,128)(2,1)S(1)}, bf16[1,16,32,128]{3,2,1,0:T(8,128)(2,1)}, u32[]{:S(2)}) copy-start(bf16[1,16,32,128]{3,2,1,0:T(8,128)(2,1)} %param.14) | copy-start | bytes 393220
  7.7 5.0 %collective-permute-start.4 = (bf16[512,128]{1,0:T(8,128)(2,1)S(1)}, bf16[512,128]{1,0:T(8,128)(2,1)S(1)}, u32[]{:S(2)}, u32[]{:S(2)}) collective-permute-start(bf16[512,128]{1,0:T(8,128)(2,1)S(1)} %pad_maximum_fusion.2), channel_id=1, source_target_pairs={{0,2},{1,3},{2,0},{3,1},{4,6},{5,7},{6,4},{7,5},{8,10},{9,11},{10,... | collective-permute-start | bytes 393224 | tf_op jit(solution)/shard_map/ppermute | solution.py:330
  8.9 0.7 %copy-start.4 = (f32[1,4,256]{2,1,0:T(4,128)S(1)}, f32[1,4,256]{2,1,0:T(4,128)}, u32[]{:S(2)}) copy-start(f32[1,4,256]{2,1,0:T(4,128)} %refs_1_.2) | copy-start | bytes 12292
  9.6 0.7 %copy-start.5 = (s32[1,256]{1,0:T(1,128)S(1)}, s32[1,256]{1,0:T(1,128)}, u32[]{:S(2)}) copy-start(s32[1,256]{1,0:T(1,128)} %refs_0_.3) | copy-start | bytes 3076
  12.1 4.4 %collective-permute-start.3 = (bf16[1024,128]{1,0:T(8,128)(2,1)S(1)}, bf16[1024,128]{1,0:T(8,128)(2,1)S(1)}, u32[]{:S(2)}, u32[]{:S(2)}) collective-permute-start(bf16[1024,128]{1,0:T(8,128)(2,1)S(1)} %get-tuple-element.13.refs_3_), channel_id=1, source_target_pairs={{0,1},{1,0},{2,3},{3,2},{4,5},{5,4},{6,7},{7,6},{8,9},{9,8},{10,11... | collective-permute-start | bytes 786440 | tf_op jit(solution)/shard_map/ppermute | solution.py:330
  12.8 3.7 %collective-permute-start.5 = (bf16[512,128]{1,0:T(8,128)(2,1)S(1)}, bf16[512,128]{1,0:T(8,128)(2,1)S(1)}, u32[]{:S(2)}, u32[]{:S(2)}) collective-permute-start(bf16[512,128]{1,0:T(8,128)(2,1)S(1)} %collective-permute-done.4.refs_5_), channel_id=1, source_target_pairs={{0,1},{1,0},{2,3},{3,2},{4,5},{5,4},{6,7},{7,6},{8,9},{9,8},{10,11... | collective-permute-start | bytes 393224 | tf_op jit(solution)/shard_map/ppermute | solution.py:330
  12.8 11.7 %collective-permute-start.8 = (bf16[1024,128]{1,0:T(8,128)(2,1)S(1)}, bf16[1024,128]{1,0:T(8,128)(2,1)S(1)}, u32[]{:S(2)}, u32[]{:S(2)}) collective-permute-start(bf16[1024,128]{1,0:T(8,128)(2,1)S(1)} %pad_maximum_fusion.1), channel_id=1, source_target_pairs={{0,4},{1,5},{2,6},{3,7},{4,0},{5,1},{6,2},{7,3},{8,12},{9,13},{10,... | collective-permute-start | bytes 786440 | tf_op jit(solution)/shard_map/ppermute | solution.py:327
  14.4 10.1 %collective-permute-start.9 = (bf16[1024,128]{1,0:T(8,128)(2,1)S(1)}, bf16[1024,128]{1,0:T(8,128)(2,1)S(1)}, u32[]{:S(2)}, u32[]{:S(2)}) collective-permute-start(bf16[1024,128]{1,0:T(8,128)(2,1)S(1)} %pad_maximum_fusion.1), channel_id=1, source_target_pairs={{0,1},{1,0},{2,3},{3,2},{4,8},{5,9},{6,10},{7,11},{8,4},{9,5},{10,... | collective-permute-start | bytes 786440 | tf_op jit(solution)/shard_map/ppermute | solution.py:327
  31.4 1.4 %collective-permute-start.10 = (f32[2,128,128]{2,1,0:T(8,128)S(1)}, f32[2,128,128]{2,1,0:T(8,128)S(1)}, u32[]{:S(2)}, u32[]{:S(2)}) collective-permute-start(f32[2,128,128]{2,1,0:T(8,128)S(1)} %slice.13), channel_id=1, source_target_pairs={{0,1},{1,0},{2,3},{3,2},{4,5},{5,4},{6,7},{7,6},{8,9},{9,8},{10,11... | collective-permute-start | bytes 393224 | tf_op jit(solution)/shard_map/ppermute | solution.py:330
  32.8 4.3 %collective-permute-start.11 = (f32[1,128,128]{2,1,0:T(8,128)S(1)}, f32[1,128,128]{2,1,0:T(8,128)S(1)}, u32[]{:S(2)}, u32[]{:S(2)}) collective-permute-start(f32[1,128,128]{2,1,0:T(8,128)S(1)} %slice.17), channel_id=1, source_target_pairs={{0,2},{1,3},{2,0},{3,1},{4,6},{5,7},{6,4},{7,5},{8,10},{9,11},{10,... | collective-permute-start | bytes 196616 | tf_op jit(solution)/shard_map/ppermute | solution.py:330
